TPU v7x, 32 devices: a whole 2x2x4 slice. The times are simulated.
32 devices in a mesh: parts: 2 (over x), leaf: 16 (over z, y, core).
Axes of the slice: x: 2, y: 2, z: 4, core: 2. Of those that a mesh axis runs over, the one named last changes fastest.
Arguments:
- rhs: bfloat16 [131072, 384], P(('parts', 'leaf')), parts along dimension 0, may hold values from -6 to 6
- left_basis: bfloat16 [2, 131072, 64], P(None, ('parts', 'leaf')), parts along dimension 1, may hold values from -0.0625 to 0.0625
- right_basis: bfloat16 [2, 131072, 64], P(None, ('parts', 'leaf')), parts along dimension 1, may hold values from -0.5 to 0.5
- near_field: bfloat16 [2, 512, 256, 256], P(None, ('parts', 'leaf')), parts along dimension 1, may hold values from -0.25 to 0.25
- factors: bfloat16 [32, 4, 2, 2, 64, 64], P(('parts', 'leaf')), parts along dimension 0, may hold values from -0.375 to 0.375
- coupling: bfloat16 [32, 16, 2, 64, 64], P(('parts', 'leaf')), parts along dimension 0, may hold values from -0.125 to 0.125
- pattern: int32 [32, 4, 4], P(('parts', 'leaf')), parts along dimension 0, may hold values 0 or 1
- leaf_order: int32 [32, 16], P(('parts', 'leaf')), parts along dimension 0, may hold values from 0 to 15, each once within a row
Outputs:
- product: bfloat16 [131072, 384], P(('parts', 'leaf')), parts along dimension 0
There are 2 independent parts, one for each index of `parts`. A program takes and returns all parts, laid end to end along the dimension named above; each array names one. Nothing has to cross between parts.
Inputs may be any that keep to these rules, and one draw needn't show every extreme that they name: `leaf_order`: each row names every slot of the group exactly once.
All inputs are finite; a program needn't handle non-finite values. No bound on the sum of `pattern` on one device may be relied on, other than what follows from the above.
Results may differ from a plain program's by a relative error of at most 0.0065.
Values may be sent and summed in bfloat16 or wider, within the bound.
No kernel may reach another device: no remote copies, remote signals or barrier semaphores. Data moves between devices by JAX's collectives and lax.ppermute only.
A program may use at most 128 MiB of HBM per device.

v0:
```python
import jax
import jax.numpy as jnp
from jax import lax
from jax.sharding import PartitionSpec as P


def swapped(array, axis, apart):
    return lax.ppermute(array, axis, [(i, i ^ 1 << apart) for i in range(lax.axis_size(axis))])


def combine(prod_re, prod_im, half_cols):
    real_part = prod_re[..., :half_cols] - prod_im[..., half_cols:]
    imag_part = prod_re[..., half_cols:] + prod_im[..., :half_cols]
    return jnp.concatenate([real_part, imag_part], axis=-1)


def complex_apply(matrix_re, matrix_im, vectors, half_cols):
    part_re = jnp.dot(matrix_re, vectors, preferred_element_type=jnp.float32)
    part_im = jnp.dot(matrix_im, vectors, preferred_element_type=jnp.float32)
    return combine(part_re, part_im, half_cols)


def per_device(rhs, left_basis, right_basis, near_field, factors, coupling, pattern, leaf_order):
    half_cols = rhs.shape[1] // 2
    rank_width = left_basis.shape[2]
    row_count = rhs.shape[0]
    dims = (((0,), (0,)), ((), ()))
    skeleton = combine(
        lax.dot_general(left_basis[0], rhs, dims, preferred_element_type=jnp.float32),
        lax.dot_general(left_basis[1], rhs, dims, preferred_element_type=jnp.float32),
        half_cols,
    ).astype(jnp.bfloat16)
    bit_count = lax.axis_size("leaf").bit_length() - 1
    blocks = pattern.shape[2]
    for level_idx in range(factors.shape[1]):
        partner = swapped(skeleton, "leaf", bit_count - 1 - level_idx)
        row_mask = jnp.repeat(pattern[0, level_idx], rank_width // blocks).astype(jnp.bfloat16)
        self_factor = factors[0, level_idx, 0]
        cross_factor = factors[0, level_idx, 1] * row_mask[None, :, None]
        mixed_sum = complex_apply(
            self_factor[0], self_factor[1], skeleton, half_cols
        ) + complex_apply(cross_factor[0], cross_factor[1], partner, half_cols)
        skeleton = mixed_sum.astype(jnp.bfloat16)
    group_size = leaf_order.shape[1]
    leaf_index = lax.axis_index("leaf")
    members = skeleton[None]
    for bit_idx in range(group_size.bit_length() - 1):
        partner_block = swapped(members, "leaf", bit_idx)
        lower_half = leaf_index >> bit_idx & 1 == 0
        members = jnp.where(
            lower_half,
            jnp.concatenate([members, partner_block], axis=0),
            jnp.concatenate([partner_block, members], axis=0),
        )
    chosen = jnp.take(members, leaf_order[0], axis=0)
    couple = coupling[0]
    part_re = jnp.einsum("jik,jkc->ic", couple[:, 0], chosen, preferred_element_type=jnp.float32)
    part_im = jnp.einsum("jik,jkc->ic", couple[:, 1], chosen, preferred_element_type=jnp.float32)
    coarse = combine(part_re, part_im, half_cols).astype(jnp.bfloat16)
    far_field = complex_apply(right_basis[0], right_basis[1], coarse, half_cols)
    box_count = near_field.shape[1]
    box_width = near_field.shape[2]
    rhs_boxes = rhs.reshape(box_count, box_width, rhs.shape[1])
    near_term = combine(
        jnp.einsum("bij,bjc->bic", near_field[0], rhs_boxes, preferred_element_type=jnp.float32),
        jnp.einsum("bij,bjc->bic", near_field[1], rhs_boxes, preferred_element_type=jnp.float32),
        half_cols,
    ).reshape(row_count, rhs.shape[1])
    return (far_field + near_term).astype(jnp.bfloat16)


def solution(mesh):
    in_specs = (
        P(("parts", "leaf"), None),
        P(None, ("parts", "leaf"), None),
        P(None, ("parts", "leaf"), None),
        P(None, ("parts", "leaf"), None, None),
        P(("parts", "leaf"), None, None, None, None, None),
        P(("parts", "leaf"), None, None, None, None),
        P(("parts", "leaf"), None, None),
        P(("parts", "leaf"), None),
    )
    out_specs = P(("parts", "leaf"), None)
    return jax.shard_map(
        per_device, mesh=mesh, in_specs=in_specs, out_specs=out_specs, check_vma=False
    )
```

profile of v0, /device:TPU:0, one launch (start us, length us, event | category | flops | bytes accessed | tf_op | source)
XLA Modules:
  0.0 95.6 jit_solution(10318942526661590545)
XLA Ops:
  0.0 1.9 %copy-done = bf16[4096,384]{1,0:T(8,128)(2,1)S(1)} copy-done((bf16[4096,384]{1,0:T(8,128)(2,1)S(1)}, bf16[4096,384]{1,0:T(8,128)(2,1)}, u32[]{:S(2)}) %copy-start) | copy-done | bytes 3145752
  1.9 1.6 %fusion.9 = f32[64,384]{1,0:T(8,128)S(1)} fusion(bf16[4096,384]{1,0:T(8,128)(2,1)S(1)} %copy-done, bf16[2,4096,64]{1,2,0:T(8,128)(2,1)} %param.9), kind=kOutput, calls=%fused_computation.30 | convolution fusion | flops 201326592 | bytes 3768320 | tf_op jit(solution)/shard_map/dot_general | solution.py:30
  3.5 1.6 %fusion.11 = f32[64,384]{1,0:T(8,128)S(1)} fusion(bf16[4096,384]{1,0:T(8,128)(2,1)S(1)} %copy-done, bf16[2,4096,64]{1,2,0:T(8,128)(2,1)} %param.9), kind=kOutput, calls=%fused_computation.32 | convolution fusion | flops 201326592 | bytes 3768320 | tf_op jit(solution)/shard_map/dot_general | solution.py:29
  5.3 4.1 %collective-permute-start = (bf16[64,384]{1,0:T(8,128)(2,1)S(1)}, bf16[64,384]{1,0:T(8,128)(2,1)S(1)}, u32[]{:S(2)}, u32[]{:S(2)}) collective-permute-start(bf16[64,384]{1,0:T(8,128)(2,1)S(1)} %pad_maximum_fusion.1), channel_id=1, source_target_pairs={{0,8},{1,9},{2,10},{3,11},{4,12},{5,13},{6,14},{7,15},{8,0},{9,1},... | collective-permute-start | bytes 147464 | tf_op jit(solution)/shard_map/ppermute | solution.py:8
  9.4 0.9 convolution_bitcast_fusion.10
  10.3 0.9 convolution_bitcast_fusion.11
  11.8 5.5 %fusion.1 = f32[16,256,384]{2,1,0:T(8,128)} fusion(bf16[16,256,384]{2,1,0:T(8,128)(2,1)S(1)} %bitcast.156, bf16[2,16,256,256]{3,2,1,0:T(8,128)(2,1)} %param.11), kind=kOutput, calls=%fused_computation.10 | convolution fusion | flops 805306368 | bytes 11534336 | tf_op jit(solution)/shard_map/bij,bjc->bic/dot_general | solution.py:66
  17.4 0.1 bitcast_multiply_fusion
  17.6 0.1 fusion.35
  17.7 0.1 fusion.36
  18.1 0.1 convolution_bitcast_fusion.8
  18.2 0.1 convolution_bitcast_fusion.9
  18.3 1.6 %collective-permute-start.1 = (bf16[64,384]{1,0:T(8,128)(2,1)S(1)}, bf16[64,384]{1,0:T(8,128)(2,1)S(1)}, u32[]{:S(2)}, u32[]{:S(2)}) collective-permute-start(bf16[64,384]{1,0:T(8,128)(2,1)S(1)} %fusion.17), channel_id=1, source_target_pairs={{0,4},{1,5},{2,6},{3,7},{4,0},{5,1},{6,2},{7,3},{8,12},{9,13},{10,... | collective-permute-start | bytes 147464 | tf_op jit(solution)/shard_map/ppermute | solution.py:8
  20.1 2.4 %collective-permute-done.1 = bf16[64,384]{1,0:T(8,128)(2,1)S(1)} collective-permute-done((bf16[64,384]{1,0:T(8,128)(2,1)S(1)}, bf16[64,384]{1,0:T(8,128)(2,1)S(1)}, u32[]{:S(2)}, u32[]{:S(2)}) %collective-permute-start.1) | collective-permute-done | bytes 49184 | tf_op jit(solution)/shard_map/ppermute | solution.py:8
  22.5 0.1 fusion.33
  22.6 0.1 fusion.34
  22.8 0.1 slice_subtract_fusion.7
  23.0 0.1 convolution_bitcast_fusion.6
  23.1 0.1 convolution_bitcast_fusion.7
  23.3 1.6 %collective-permute-start.2 = (bf16[64,384]{1,0:T(8,128)(2,1)S(1)}, bf16[64,384]{1,0:T(8,128)(2,1)S(1)}, u32[]{:S(2)}, u32[]{:S(2)}) collective-permute-start(bf16[64,384]{1,0:T(8,128)(2,1)S(1)} %fusion.18), channel_id=1, source_target_pairs={{0,2},{1,3},{2,0},{3,1},{4,6},{5,7},{6,4},{7,5},{8,10},{9,11},{10,... | collective-permute-start | bytes 147464 | tf_op jit(solution)/shard_map/ppermute | solution.py:8
  25.0 2.5 %collective-permute-done.2 = bf16[64,384]{1,0:T(8,128)(2,1)S(1)} collective-permute-done((bf16[64,384]{1,0:T(8,128)(2,1)S(1)}, bf16[64,384]{1,0:T(8,128)(2,1)S(1)}, u32[]{:S(2)}, u32[]{:S(2)}) %collective-permute-start.2) | collective-permute-done | bytes 49184 | tf_op jit(solution)/shard_map/ppermute | solution.py:8
  27.4 0.1 fusion.31
  27.6 0.1 fusion.32
  27.7 0.1 slice_subtract_fusion.5
  27.9 0.1 convolution_bitcast_fusion.4
  28.1 0.1 convolution_bitcast_fusion.5
  28.4 1.1 %collective-permute-done.3 = bf16[64,384]{1,0:T(8,128)(2,1)S(1)} collective-permute-done((bf16[64,384]{1,0:T(8,128)(2,1)S(1)}, bf16[64,384]{1,0:T(8,128)(2,1)S(1)}, u32[]{:S(2)}, u32[]{:S(2)}) %collective-permute-start.3) | collective-permute-done | bytes 49184 | tf_op jit(solution)/shard_map/ppermute | solution.py:8
  29.5 0.1 fusion.29
  29.6 0.1 fusion.30
  30.0 0.2 collective-permute-start.4
  30.2 3.8 %fusion.3 = f32[16,256,384]{2,1,0:T(8,128)} fusion(bf16[16,256,384]{2,1,0:T(8,128)(2,1)S(1)} %bitcast.155, bf16[2,16,256,256]{3,2,1,0:T(8,128)(2,1)S(1)} %copy-done.2), kind=kOutput, calls=%fused_computation.12 | convolution fusion | flops 805306368 | bytes 11534336 | tf_op jit(solution)/shard_map/bij,bjc->bic/dot_general | solution.py:65
  34.1 1.6 %collective-permute-start.5 = (bf16[2,64,384]{2,1,0:T(8,128)(2,1)S(1)}, bf16[2,64,384]{2,1,0:T(8,128)(2,1)S(1)}, u32[]{:S(2)}, u32[]{:S(2)}) collective-permute-start(bf16[2,64,384]{2,1,0:T(8,128)(2,1)S(1)} %maximum_select_fusion.3), channel_id=1, source_target_pairs={{0,2},{1,3},{2,0},{3,1},{4,6},{5,7},{6,4},{7,5},{8,10},{9,11},{10,... | collective-permute-start | bytes 294920 | tf_op jit(solution)/shard_map/ppermute | solution.py:8
  35.7 11.3 %slice_subtract_fusion = (f32[16,256,192]{2,1,0:T(8,128)}, f32[16,256,192]{2,1,0:T(8,128)}) fusion(f32[16,256,384]{2,1,0:T(8,128)} %fusion.1, f32[16,256,384]{2,1,0:T(8,128)} %fusion.3), kind=kLoop, calls=%fused_computation.7 | loop fusion | flops 1572864 | bytes 18874368 | tf_op jit(solution)/shard_map/sub | solution.py:12
  47.0 1.6 %collective-permute-start.6 = (bf16[4,64,384]{2,1,0:T(8,128)(2,1)S(1)}, bf16[4,64,384]{2,1,0:T(8,128)(2,1)S(1)}, u32[]{:S(2)}, u32[]{:S(2)}) collective-permute-start(bf16[4,64,384]{2,1,0:T(8,128)(2,1)S(1)} %maximum_select_fusion.2), channel_id=1, source_target_pairs={{0,4},{1,5},{2,6},{3,7},{4,0},{5,1},{6,2},{7,3},{8,12},{9,13},{10,... | collective-permute-start | bytes 589832 | tf_op jit(solution)/shard_map/ppermute | solution.py:8
  48.6 7.4 %pad_maximum_fusion = f32[16,256,384]{2,1,0:T(8,128)} fusion(f32[16,256,192]{2,1,0:T(8,128)} %get-tuple-element.8, f32[16,256,192]{2,1,0:T(8,128)} %get-tuple-element.7), kind=kLoop, calls=%fused_computation.3 | loop fusion | flops 1572864 | bytes 12582912 | tf_op jit(solution)/shard_map/concatenate | solution.py:14
  56.1 0.4 collective-permute-start.7
  56.5 6.7 %copy.12 = f32[4096,384]{0,1:T(8,128)} copy(f32[4096,384]{1,0:T(8,128)} %bitcast.157) | data formatting | bytes 12582912 | tf_op jit(solution)/shard_map/reshape | solution.py:68
  63.3 0.8 copy.14
  64.1 12.1 %collective-permute-done.7 = bf16[8,64,384]{2,1,0:T(8,128)(2,1)S(1)} collective-permute-done((bf16[8,64,384]{2,1,0:T(8,128)(2,1)S(1)}, bf16[8,64,384]{2,1,0:T(8,128)(2,1)S(1)}, u32[]{:S(2)}, u32[]{:S(2)}) %collective-permute-start.7) | collective-permute-done | bytes 393248 | tf_op jit(solution)/shard_map/ppermute | solution.py:8
  76.2 0.1 maximum_select_fusion
  76.4 0.7 gather_fusion
  77.1 1.3 %convolution_bitcast_fusion.2 = f32[64,384]{1,0:T(8,128)S(1)} fusion(bf16[16,64,384]{2,1,0:T(8,128)(2,1)S(1)} %gather_fusion, pred[16]{0:T(512)(128)(4,1)S(1)} %compare_and_fusion, bf16[16,2,64,64]{3,2,0,1:T(8,128)(2,1)} %bitcast.158), kind=kOutput, calls=%fused_computation.16 | convolution fusion | flops 50724864 | bytes 1146896 | tf_op jit(solution)/shard_map/jik,jkc->ic/dot_general | solution.py:58
  78.4 1.3 %convolution_bitcast_fusion.3 = f32[64,384]{1,0:T(8,128)S(1)} fusion(bf16[16,64,384]{2,1,0:T(8,128)(2,1)S(1)} %gather_fusion, pred[16]{0:T(512)(128)(4,1)S(1)} %compare_and_fusion, bf16[16,2,64,64]{3,2,0,1:T(8,128)(2,1)} %bitcast.159), kind=kOutput, calls=%fused_computation.17 | convolution fusion | flops 50724864 | bytes 1146896 | tf_op jit(solution)/shard_map/jik,jkc->ic/dot_general | solution.py:57
  79.8 1.0 %convolution_bitcast_fusion = f32[4096,384]{0,1:T(8,128)S(1)} fusion(bf16[2,4096,64]{1,2,0:T(8,128)(2,1)S(1)} %copy-done.3, bf16[64,192]{1,0:T(8,128)(2,1)S(1)} %get-tuple-element.14, bf16[64,192]{1,0:T(8,128)(2,1)S(1)} %get-tuple-element.13), kind=kOutput, calls=%fused_computation.4 | convolution fusion | flops 201424896 | bytes 6881280 | tf_op jit(solution)/shard_map/dot_general | solution.py:19
  80.8 1.0 %convolution_bitcast_fusion.1 = f32[4096,384]{0,1:T(8,128)S(1)} fusion(bf16[2,4096,64]{1,2,0:T(8,128)(2,1)S(1)} %copy-done.3, bf16[64,192]{1,0:T(8,128)(2,1)S(1)} %get-tuple-element.14, bf16[64,192]{1,0:T(8,128)(2,1)S(1)} %get-tuple-element.13), kind=kOutput, calls=%fused_computation.5 | convolution fusion | flops 201424896 | bytes 6881280 | tf_op jit(solution)/shard_map/dot_general | solution.py:18
  81.8 2.8 %slice_subtract_fusion.1 = (f32[4096,192]{0,1:T(8,128)S(1)}, f32[4096,192]{0,1:T(8,128)}) fusion(f32[4096,384]{0,1:T(8,128)S(1)} %convolution_bitcast_fusion, f32[4096,384]{0,1:T(8,128)S(1)} %convolution_bitcast_fusion.1), kind=kLoop, calls=%fused_computation.9 | loop fusion | flops 1572864 | bytes 18874368 | tf_op jit(solution)/shard_map/sub | solution.py:12
  84.6 6.3 %fusion = bf16[4096,384]{0,1:T(8,128)(2,1)} fusion(f32[4096,384]{0,1:T(8,128)} %copy.12, f32[4096,192]{0,1:T(8,128)} %get-tuple-element.6, f32[4096,192]{0,1:T(8,128)S(1)} %get-tuple-element.5), kind=kLoop, calls=%fused_computation.2 | loop fusion | flops 4718592 | bytes 15728640 | tf_op jit(solution)/shard_map/convert_element_type | solution.py:69
  90.9 4.6 %copy.11 = bf16[4096,384]{1,0:T(8,128)(2,1)} copy(bf16[4096,384]{0,1:T(8,128)(2,1)} %fusion) | data formatting | bytes 6291456 | tf_op jit(solution)/shard_map/convert_element_type | solution.py:69
  (49 shorter events, 2.2 us)
Async XLA Ops:
  0.0 1.9 %copy-start = (bf16[4096,384]{1,0:T(8,128)(2,1)S(1)}, bf16[4096,384]{1,0:T(8,128)(2,1)}, u32[]{:S(2)}) copy-start(bf16[4096,384]{1,0:T(8,128)(2,1)} %param.8) | copy-start | bytes 9437188
  0.0 11.1 %copy-start.6 = (s32[1,4,4]{2,1,0:T(4,128)S(1)}, s32[1,4,4]{2,1,0:T(4,128)}, u32[]{:S(2)}) copy-start(s32[1,4,4]{2,1,0:T(4,128)} %param.14) | copy-start | bytes 196
  5.3 12.2 %collective-permute-start = (bf16[64,384]{1,0:T(8,128)(2,1)S(1)}, bf16[64,384]{1,0:T(8,128)(2,1)S(1)}, u32[]{:S(2)}, u32[]{:S(2)}) collective-permute-start(bf16[64,384]{1,0:T(8,128)(2,1)S(1)} %pad_maximum_fusion.1), channel_id=1, source_target_pairs={{0,8},{1,9},{2,10},{3,11},{4,12},{5,13},{6,14},{7,15},{8,0},{9,1},... | collective-permute-start | bytes 147464 | tf_op jit(solution)/shard_map/ppermute | solution.py:8
  11.8 5.6 %copy-start.5 = (bf16[1,4,2,2,64,64]{5,4,3,2,1,0:T(8,128)(2,1)S(1)}, bf16[1,4,2,2,64,64]{5,4,3,2,1,0:T(8,128)(2,1)}, u32[]{:S(2)}) copy-start(bf16[1,4,2,2,64,64]{5,4,3,2,1,0:T(8,128)(2,1)} %param.12) | copy-start | bytes 393220
  17.3 12.9 %copy-start.2 = (bf16[2,16,256,256]{3,2,1,0:T(8,128)(2,1)S(1)}, bf16[2,16,256,256]{3,2,1,0:T(8,128)(2,1)}, u32[]{:S(2)}) copy-start(bf16[2,16,256,256]{3,2,1,0:T(8,128)(2,1)} %param.11) | copy-start | bytes 12582916
  18.3 4.2 %collective-permute-start.1 = (bf16[64,384]{1,0:T(8,128)(2,1)S(1)}, bf16[64,384]{1,0:T(8,128)(2,1)S(1)}, u32[]{:S(2)}, u32[]{:S(2)}) collective-permute-start(bf16[64,384]{1,0:T(8,128)(2,1)S(1)} %fusion.17), channel_id=1, source_target_pairs={{0,4},{1,5},{2,6},{3,7},{4,0},{5,1},{6,2},{7,3},{8,12},{9,13},{10,... | collective-permute-start | bytes 147464 | tf_op jit(solution)/shard_map/ppermute | solution.py:8
  23.3 4.2 %collective-permute-start.2 = (bf16[64,384]{1,0:T(8,128)(2,1)S(1)}, bf16[64,384]{1,0:T(8,128)(2,1)S(1)}, u32[]{:S(2)}, u32[]{:S(2)}) collective-permute-start(bf16[64,384]{1,0:T(8,128)(2,1)S(1)} %fusion.18), channel_id=1, source_target_pairs={{0,2},{1,3},{2,0},{3,1},{4,6},{5,7},{6,4},{7,5},{8,10},{9,11},{10,... | collective-permute-start | bytes 147464 | tf_op jit(solution)/shard_map/ppermute | solution.py:8
  28.2 1.3 %collective-permute-start.3 = (bf16[64,384]{1,0:T(8,128)(2,1)S(1)}, bf16[64,384]{1,0:T(8,128)(2,1)S(1)}, u32[]{:S(2)}, u32[]{:S(2)}) collective-permute-start(bf16[64,384]{1,0:T(8,128)(2,1)S(1)} %fusion.19), channel_id=1, source_target_pairs={{0,1},{1,0},{2,3},{3,2},{4,5},{5,4},{6,7},{7,6},{8,9},{9,8},{10,11... | collective-permute-start | bytes 147464 | tf_op jit(solution)/shard_map/ppermute | solution.py:8
  30.0 4.1 %collective-permute-start.4 = (bf16[1,64,384]{2,1,0:T(8,128)(2,1)S(1)}, bf16[1,64,384]{2,1,0:T(8,128)(2,1)S(1)}, u32[]{:S(2)}, u32[]{:S(2)}) collective-permute-start(bf16[1,64,384]{2,1,0:T(8,128)(2,1)S(1)} %fusion.20), channel_id=1, source_target_pairs={{0,1},{1,0},{2,3},{3,2},{4,5},{5,4},{6,7},{7,6},{8,9},{9,8},{10,11... | collective-permute-start | bytes 147464 | tf_op jit(solution)/shard_map/ppermute | solution.py:8
  34.1 12.9 %collective-permute-start.5 = (bf16[2,64,384]{2,1,0:T(8,128)(2,1)S(1)}, bf16[2,64,384]{2,1,0:T(8,128)(2,1)S(1)}, u32[]{:S(2)}, u32[]{:S(2)}) collective-permute-start(bf16[2,64,384]{2,1,0:T(8,128)(2,1)S(1)} %maximum_select_fusion.3), channel_id=1, source_target_pairs={{0,2},{1,3},{2,0},{3,1},{4,6},{5,7},{6,4},{7,5},{8,10},{9,11},{10,... | collective-permute-start | bytes 294920 | tf_op jit(solution)/shard_map/ppermute | solution.py:8
  47.0 9.1 %collective-permute-start.6 = (bf16[4,64,384]{2,1,0:T(8,128)(2,1)S(1)}, bf16[4,64,384]{2,1,0:T(8,128)(2,1)S(1)}, u32[]{:S(2)}, u32[]{:S(2)}) collective-permute-start(bf16[4,64,384]{2,1,0:T(8,128)(2,1)S(1)} %maximum_select_fusion.2), channel_id=1, source_target_pairs={{0,4},{1,5},{2,6},{3,7},{4,0},{5,1},{6,2},{7,3},{8,12},{9,13},{10,... | collective-permute-start | bytes 589832 | tf_op jit(solution)/shard_map/ppermute | solution.py:8
  48.6 7.9 %copy-start.7 = (s32[1,16]{1,0:T(1,128)S(1)}, s32[1,16]{1,0:T(1,128)}, u32[]{:S(2)}) copy-start(s32[1,16]{1,0:T(1,128)} %param.15) | copy-start | bytes 196
  56.1 20.1 %collective-permute-start.7 = (bf16[8,64,384]{2,1,0:T(8,128)(2,1)S(1)}, bf16[8,64,384]{2,1,0:T(8,128)(2,1)S(1)}, u32[]{:S(2)}, u32[]{:S(2)}) collective-permute-start(bf16[8,64,384]{2,1,0:T(8,128)(2,1)S(1)} %maximum_select_fusion.1), channel_id=1, source_target_pairs={{0,8},{1,9},{2,10},{3,11},{4,12},{5,13},{6,14},{7,15},{8,0},{9,1},... | collective-permute-start | bytes 1179656 | tf_op jit(solution)/shard_map/ppermute | solution.py:8
  56.5 6.7 %copy-start.4 = (bf16[1,16,2,64,64]{4,3,2,1,0:T(8,128)(2,1)S(1)}, bf16[1,16,2,64,64]{4,3,2,1,0:T(8,128)(2,1)}, u32[]{:S(2)}) copy-start(bf16[1,16,2,64,64]{4,3,2,1,0:T(8,128)(2,1)} %param.13) | copy-start | bytes 786436
  63.3 16.5 %copy-start.3 = (bf16[2,4096,64]{1,2,0:T(8,128)(2,1)S(1)}, bf16[2,4096,64]{1,2,0:T(8,128)(2,1)}, u32[]{:S(2)}) copy-start(bf16[2,4096,64]{1,2,0:T(8,128)(2,1)} %param.10) | copy-start | bytes 3145732
  84.6 11.0 %copy-start.1 = (bf16[4096,384]{1,0:T(8,128)(2,1)S(1)}, bf16[4096,384]{1,0:T(8,128)(2,1)}, u32[]{:S(2)}) copy-start(bf16[4096,384]{1,0:T(8,128)(2,1)} %param.8) | copy-start | bytes 9437188
where the time goes:
time: 96.1 us; the launch traced here: 95.6 us
  other arithmetic  29.6 us (31%)
  matrix products  20.8 us (22%)
  waiting for transfers between devices  18.1 us (19%)
  local copies, waits for them, and re-layouts  15.5 us (16%)
  starting transfers between devices  11.2 us (12%)
    ppermute x8, waiting for transfers between devices, swapped(): lax.ppermute(array, axis, [(i, i ^ 1 << apart) for i in range(lax.axis_si...  18.1 us
    sub x8, other arithmetic, combine(): real_part = prod_re[..., :half_cols] - prod_im[..., half_cols:]  14.6 us
    ppermute x8, starting transfers between devices, swapped(): lax.ppermute(array, axis, [(i, i ^ 1 << apart) for i in range(lax.axis_si...  11.2 us
    concatenate x4, other arithmetic, combine(): return jnp.concatenate([real_part, imag_part], axis=-1)  7.69 us
    reshape x1, local copies, waits for them, and re-layouts, per_device(): near_term = combine(jnp.einsum('bij,bjc->bic', near_field[0], rhs_boxes,...  6.73 us
    convert_element_type x1, other arithmetic, per_device(): return (far_field + near_term).astype(jnp.bfloat16)  6.34 us
    dot_general x1, matrix products, per_device(): jnp.einsum('bij,bjc->bic', near_field[1], rhs_boxes, preferred_element_ty...  5.52 us
    convert_element_type x1, local copies, waits for them, and re-layouts, per_device(): return (far_field + near_term).astype(jnp.bfloat16)  4.63 us
  transfers between devices with their start and end apart: 8, of which 4 were waited for; matrix products, arithmetic and copies ran while one was open for 40% of the time, Pallas kernels for 0%

commit v1 on v0

v1 whole, which is shorter than its diff:
```python
import functools

import jax
import jax.numpy as jnp
from jax import lax
from jax.experimental import pallas as pl
from jax.experimental.pallas import tpu as pltpu
from jax.sharding import PartitionSpec as P

BF = jnp.bfloat16
F32 = jnp.float32
VMEM = pl.BlockSpec(memory_space=pltpu.VMEM)
SMEM = pl.BlockSpec(memory_space=pltpu.SMEM)
ANY = pl.BlockSpec(memory_space=pl.ANY)
HBM = pl.BlockSpec(memory_space=pltpu.HBM)


def partner(array, apart):
    count = lax.axis_size("leaf")
    return lax.ppermute(array, "leaf", [(i, i ^ apart) for i in range(count)])


def in_hbm(array):
    return pltpu.with_memory_space_constraint(array, pltpu.HBM)


def turned(block):
    half = block.shape[1] // 2
    return jnp.concatenate([-block[:, half:], block[:, :half]], axis=1)


def combined(stacked):
    rank = stacked.shape[0] // 2
    return stacked[:rank] + turned(stacked[rank:])


def dot(a, b):
    return jnp.dot(a, b, preferred_element_type=F32)


def params(mib):
    return pltpu.CompilerParams(vmem_limit_bytes=mib * 2**20)


def cost(flops, moved):
    return pl.CostEstimate(flops=flops, bytes_accessed=moved, transcendentals=0)


def project_kernel(chunks, left, rhs, factors, pattern, skel, rhs_keep, mixers, left_buf, fac_buf, sems):
    depth = rhs.shape[0] // chunks
    rank = left.shape[1]
    fac_copy = pltpu.make_async_copy(factors, fac_buf, sems.at[2 * chunks])
    copies = []
    for c in range(chunks):
        span = pl.ds(c * depth, depth)
        copies.append((
            pltpu.make_async_copy(left.at[:, :, span], left_buf.at[:, :, span], sems.at[2 * c]),
            pltpu.make_async_copy(rhs.at[span], rhs_keep.at[span], sems.at[2 * c + 1]),
        ))
    for one, two in copies[:1]:
        one.start()
        two.start()
    fac_copy.start()
    for one, two in copies[1:]:
        one.start()
        two.start()
    fac_copy.wait()
    levels = factors.shape[0]
    blocks = pattern.shape[1]
    row_block = lax.broadcasted_iota(jnp.int32, (rank, rank), 0) // (rank // blocks)
    for level in range(levels):
        keep = jnp.zeros((rank, rank), F32)
        for r in range(blocks):
            keep = jnp.where(row_block == r, pattern[level, r].astype(F32), keep)
        for part in range(2):
            own = fac_buf[level, 0, part]
            cross = (fac_buf[level, 1, part].astype(F32) * keep).astype(BF)
            mixers[level, pl.ds(part * rank, rank), :] = jnp.concatenate([own, cross], axis=1)
    total = jnp.zeros((2 * rank, rhs.shape[1]), F32)
    for c in range(chunks):
        span = pl.ds(c * depth, depth)
        copies[c][0].wait()
        copies[c][1].wait()
        total += dot(left_buf[:, :, span].reshape(2 * rank, depth), rhs_keep[span, :])
    skel[...] = combined(total).astype(BF)


def project(left_t, rhs, factors, pattern):
    chunks = 8
    rank = left_t.shape[1]
    levels = factors.shape[0]
    return pl.pallas_call(
        functools.partial(project_kernel, chunks),
        out_shape=(
            pltpu.VMEM((rank, rhs.shape[1]), BF),
            pltpu.VMEM(rhs.shape, BF),
            pltpu.VMEM((levels, 2 * rank, 2 * rank), BF),
        ),
        in_specs=[HBM, HBM, HBM, SMEM],
        out_specs=(VMEM, VMEM, VMEM),
        scratch_shapes=[
            pltpu.VMEM(left_t.shape, BF),
            pltpu.VMEM(factors.shape, BF),
            pltpu.SemaphoreType.DMA((2 * chunks + 1,)),
        ],
        compiler_params=params(8),
        cost_estimate=cost(4 * left_t.size * rhs.shape[1], 2 * (left_t.size + rhs.size)),
        name="project",
    )(left_t, rhs, factors, pattern)


def near_kernel(first, near, rhs_keep, out, token, buf, sems):
    count = buf.shape[1]
    width = buf.shape[2]
    copies = []
    for b in range(count):
        copies.append(pltpu.make_async_copy(near.at[:, first + b], buf.at[:, b], sems.at[b]))
        copies[-1].start()
    for b in range(count):
        block = rhs_keep[pl.ds((first + b) * width, width), :]
        side = turned(block)
        copies[b].wait()
        out[pl.ds(b * width, width), :] = dot(buf[0, b], block) + dot(buf[1, b], side)
    token[...] = jnp.zeros_like(token)


def near_part(near, rhs_keep, first, count):
    width = near.shape[2]
    cols = rhs_keep.shape[1]
    return pl.pallas_call(
        functools.partial(near_kernel, first),
        out_shape=(pltpu.VMEM((count * width, cols), F32), jax.ShapeDtypeStruct((8, 128), F32)),
        in_specs=[HBM, VMEM],
        out_specs=(VMEM, VMEM),
        scratch_shapes=[
            pltpu.VMEM((2, count, width, width), BF),
            pltpu.SemaphoreType.DMA((count,)),
        ],
        compiler_params=params(8),
        cost_estimate=cost(4 * count * width * width * cols, 4 * count * width * width),
        name="near_part",
    )(near, rhs_keep)


def prepare_kernel(chunks, members, right, coupling, order, here, token, right_rows, table, right_buf, couple_buf, slot, sems):
    rank = right.shape[1]
    rows = right.shape[2]
    depth = rows // chunks
    group = coupling.shape[0]
    first = pltpu.make_async_copy(coupling, couple_buf, sems.at[0])
    second = pltpu.make_async_copy(right, right_buf, sems.at[1])
    first.start()
    second.start()
    for j in range(group):
        slot[order[0, j] ^ here[0]] = j
    first.wait()
    per = len(members[0])
    for row in range(len(members)):
        for part in range(2):
            pieces = [couple_buf[slot[members[row][i]], part] for i in range(per)]
            table[row, pl.ds(part * rank, rank), :] = jnp.concatenate(pieces, axis=1)
    second.wait()
    for c in range(chunks):
        span = pl.ds(c * depth, depth)
        right_rows[span, :] = right_buf[:, :, span].reshape(2 * rank, depth).T


def prepare(right_t, coupling, order, here, members, token):
    chunks = 8
    rank = right_t.shape[1]
    rows = right_t.shape[2]
    return pl.pallas_call(
        functools.partial(prepare_kernel, chunks, members),
        out_shape=(
            pltpu.VMEM((rows, 2 * rank), BF),
            pltpu.VMEM((len(members), 2 * rank, len(members[0]) * rank), BF),
        ),
        in_specs=[HBM, HBM, SMEM, SMEM, ANY],
        out_specs=(VMEM, VMEM),
        scratch_shapes=[
            pltpu.VMEM(right_t.shape, BF),
            pltpu.VMEM(coupling.shape, BF),
            pltpu.SMEM((coupling.shape[0],), jnp.int32),
            pltpu.SemaphoreType.DMA((2,)),
        ],
        compiler_params=params(8),
        cost_estimate=cost(right_t.size, 4 * right_t.size + 4 * coupling.size),
        name="prepare",
    )(right_t, coupling, order, here, token)


def level_kernel(level, mixers, skel, other, token, out):
    both = jnp.concatenate([skel[...], other[...]], axis=0)
    out[...] = combined(dot(mixers[level], both)).astype(BF)


def level_step(level, mixers, skel, other, token):
    return pl.pallas_call(
        functools.partial(level_kernel, level),
        out_shape=pltpu.VMEM(skel.shape, BF),
        in_specs=[VMEM, VMEM, VMEM, ANY],
        out_specs=VMEM,
        cost_estimate=cost(8 * skel.shape[0] * skel.size, 6 * skel.size),
        name="level_step",
    )(mixers, skel, other, token)


def fork_step(level, mixers, level_other, mixers_other, skel, other, token):
    rank, cols = skel.shape

    def kernel(mix, mix_other, own, far, token, out):
        a = own[...]
        b = far[...]
        out[:rank, :] = combined(dot(mix[level], jnp.concatenate([a, b], axis=0))).astype(BF)
        out[rank:, :] = combined(dot(mix_other[level_other], jnp.concatenate([b, a], axis=0))).astype(BF)

    return pl.pallas_call(
        kernel,
        out_shape=pltpu.VMEM((2 * rank, cols), BF),
        in_specs=[VMEM, VMEM, VMEM, VMEM, ANY],
        out_specs=VMEM,
        cost_estimate=cost(16 * rank * skel.size, 8 * skel.size),
        name="fork_step",
    )(mixers, mixers_other, skel, other, token)


def twin_step(level, mixers, level_other, mixers_other, pair, other):
    rank = pair.shape[0] // 2

    def kernel(mix, mix_other, own, far, out):
        a = own[...]
        b = far[...]
        out[:rank, :] = combined(dot(mix[level], jnp.concatenate([a[:rank], b[:rank]], axis=0))).astype(BF)
        out[rank:, :] = combined(dot(mix_other[level_other], jnp.concatenate([a[rank:], b[rank:]], axis=0))).astype(BF)

    return pl.pallas_call(
        kernel,
        out_shape=pltpu.VMEM(pair.shape, BF),
        in_specs=[VMEM, VMEM, VMEM, VMEM],
        out_specs=VMEM,
        cost_estimate=cost(16 * rank * pair.size, 8 * pair.size),
        name="twin_step",
    )(mixers, mixers_other, pair, other)


def finish_kernel(n_blocks, n_near, chunks, *refs):
    blocks = refs[:n_blocks]
    nears = refs[n_blocks:n_blocks + n_near]
    table, right_rows, out, buf, sems = refs[n_blocks + n_near:]
    per = table.shape[2] // blocks[0].shape[0]
    total = None
    for row in range(table.shape[0]):
        stack = [ref[...] for ref in blocks[row * per:(row + 1) * per]]
        both = stack[0] if per == 1 else jnp.concatenate(stack, axis=0)
        term = dot(table[row], both)
        total = term if total is None else total + term
    coarse = combined(total).astype(BF)
    weights = jnp.concatenate([coarse, turned(coarse)], axis=0)
    rows = buf.shape[0]
    depth = rows // chunks
    span_near = rows // n_near
    copies = []
    for c in range(chunks):
        span = pl.ds(c * depth, depth)
        which, at = divmod(c * depth, span_near)
        value = dot(right_rows[span, :], weights) + nears[which][pl.ds(at, depth), :]
        buf[span, :] = value.astype(BF)
        copies.append(pltpu.make_async_copy(buf.at[span], out.at[span], sems.at[c]))
        copies[-1].start()
    for copy in copies:
        copy.wait()


def finish(blocks, nears, table, right_rows):
    chunks = 8
    rows = right_rows.shape[0]
    cols = blocks[0].shape[1]
    return pl.pallas_call(
        functools.partial(finish_kernel, len(blocks), len(nears), chunks),
        out_shape=jax.ShapeDtypeStruct((rows, cols), BF),
        in_specs=[VMEM] * (len(blocks) + len(nears) + 2),
        out_specs=ANY,
        scratch_shapes=[pltpu.VMEM((rows, cols), BF), pltpu.SemaphoreType.DMA((chunks,))],
        compiler_params=params(8),
        cost_estimate=cost(2 * rows * right_rows.shape[1] * cols, 6 * rows * cols),
        name="finish",
    )(*blocks, *nears, table, right_rows)


def per_device(rhs, left_basis, right_basis, near_field, factors, coupling, pattern, leaf_order):
    leaves = lax.axis_size("leaf")
    bits = leaves.bit_length() - 1
    levels = factors.shape[1]
    group = leaf_order.shape[1]
    boxes = near_field.shape[1]
    left_t = in_hbm(jnp.swapaxes(left_basis, 1, 2))
    right_t = in_hbm(jnp.swapaxes(right_basis, 1, 2))
    near_field = in_hbm(near_field)
    couple = in_hbm(coupling[0])
    here = (lax.axis_index("leaf") % group).astype(jnp.int32)[None]

    skel, rhs_keep, mixers = project(left_t, in_hbm(rhs), in_hbm(factors[0]), pattern[0])
    parts = 4
    nears = []

    def near_next():
        value, token = near_part(near_field, rhs_keep, len(nears) * (boxes // parts), boxes // parts)
        nears.append(value)
        return token

    if leaves == group == 16 and levels == 4:
        mixers_other = partner(mixers[2:], 2)
        skel = level_step(0, mixers, skel, partner(skel, 8), near_next())
        skel = level_step(1, mixers, skel, partner(skel, 4), near_next())
        pair = fork_step(2, mixers, 0, mixers_other, skel, partner(skel, 2), near_next())
        pair = twin_step(3, mixers, 1, mixers_other, pair, partner(pair, 1))
        zs = [pair] + [partner(pair, 4 * k) for k in (3, 2, 1)]
        token = near_next()
        members = tuple((4 * k, 4 * k + 2, 4 * k + 1, 4 * k + 3) for k in (0, 3, 2, 1))
        right_rows, table = prepare(right_t, couple, leaf_order, here, members, token)
        *far, right_rows, table = lax.optimization_barrier((*zs[1:], right_rows, table))
        zs = [pair] + far
        blocks = []
        for block in zs:
            blocks += [block, partner(block, 1)]
    else:
        for level in range(levels):
            token = near_next() if len(nears) < parts else jnp.zeros((8, 128), F32)
            skel = level_step(level, mixers, skel, partner(skel, 1 << (bits - 1 - level)), token)
        while len(nears) < parts:
            token = near_next()
        blocks = [skel]
        for bit in reversed(range(group.bit_length() - 1)):
            stack = jnp.stack(blocks)
            other = partner(stack, 1 << bit)
            blocks = blocks + [other[i] for i in range(len(blocks))]
        names = [0]
        for bit in reversed(range(group.bit_length() - 1)):
            names = names + [n ^ (1 << bit) for n in names]
        members = tuple(tuple(names[i:i + 4]) for i in range(0, group, 4))
        right_rows, table = prepare(right_t, couple, leaf_order, here, members, token)
    return finish(blocks, nears, table, right_rows)


def solution(mesh):
    both = ("parts", "leaf")
    in_specs = (
        P(both, None),
        P(None, both, None),
        P(None, both, None),
        P(None, both, None, None),
        P(both, None, None, None, None, None),
        P(both, None, None, None, None),
        P(both, None, None),
        P(both, None),
    )
    return jax.shard_map(
        per_device, mesh=mesh, in_specs=in_specs, out_specs=P(both, None), check_vma=False
    )
```

time: 96.1 us -> 49.8 us (0.52)
  other arithmetic: 29.6 us -> 0 us
  Pallas kernels: 0 us -> 22.4 us
  matrix products: 20.8 us -> 0 us
  waiting for transfers between devices: 18.1 us -> 4.62 us
  local copies, waits for them, and re-layouts: 15.5 us -> 9.33 us
  starting transfers between devices: 11.2 us -> 12.9 us
    pallas_call x0 -> x11, Pallas kernels: none -> 22.4 us  [the longest x4 9.01 us: near_part(): pl.pallas_call(functools.partial(near_kernel, first), out_shape=(pltpu.VM...]
    dot_general x24 -> x0, matrix products: 20.8 us -> none  [the longest x1 5.52 us: per_device(): jnp.einsum('bij,bjc->bic', near_field[1], rhs_boxes, preferred_element_ty...]
    sub x8 -> x0, other arithmetic: 14.6 us -> none  [combine(): real_part = prod_re[..., :half_cols] - prod_im[..., half_cols:]]
    ppermute x8 -> x12, waiting for transfers between devices: 18.1 us -> 4.62 us  [partner(): return lax.ppermute(array, 'leaf', [(i, i ^ apart) for i in range(count)])]
    concatenate x4 -> x0, other arithmetic: 7.69 us -> none  [combine(): return jnp.concatenate([real_part, imag_part], axis=-1)]
    convert_element_type x5 -> x0, other arithmetic: 6.74 us -> none  [the longest x1 6.34 us: per_device(): return (far_field + near_term).astype(jnp.bfloat16)]
    reshape x1 -> x0, local copies, waits for them, and re-layouts: 6.73 us -> none  [per_device(): near_term = combine(jnp.einsum('bij,bjc->bic', near_field[0], rhs_boxes,...]
    unnamed x17 -> x42, local copies, waits for them, and re-layouts: 2.75 us -> 8.48 us
  transfers between devices with their start and end apart: 8 -> 12, of which waited for: 4 -> 5; matrix products, arithmetic and copies ran while one was open for 40% -> 2% of each run, Pallas kernels for 0% -> 25%
where the time goes in v1:
time: 49.8 us; the launch traced here: 49.5 us
  Pallas kernels  22.4 us (45%)
  starting transfers between devices  12.9 us (26%)
  local copies, waits for them, and re-layouts  9.33 us (19%)
  waiting for transfers between devices  4.62 us (9%)
    ppermute x12, starting transfers between devices, partner(): return lax.ppermute(array, 'leaf', [(i, i ^ apart) for i in range(count)])  12.9 us
    pallas_call x4, Pallas kernels, near_part(): pl.pallas_call(functools.partial(near_kernel, first), out_shape=(pltpu.VM...  9.01 us
    unnamed x42, local copies, waits for them, and re-layouts  8.48 us
    ppermute x12, waiting for transfers between devices, partner(): return lax.ppermute(array, 'leaf', [(i, i ^ apart) for i in range(count)])  4.62 us
    pallas_call x1, Pallas kernels, project(): pl.pallas_call(functools.partial(project_kernel, chunks), out_shape=(pltp...  3.66 us
    pallas_call x1, Pallas kernels, finish(): pl.pallas_call(functools.partial(finish_kernel, len(blocks), len(nears),...  2.45 us
    pallas_call x2, Pallas kernels, level_step(): pl.pallas_call(functools.partial(level_kernel, level), out_shape=pltpu.VM...  2.38 us
    pallas_call x1, Pallas kernels, prepare(): pl.pallas_call(functools.partial(prepare_kernel, chunks, members), out_sh...  2.27 us
  transfers between devices with their start and end apart: 12, of which 5 were waited for; matrix products, arithmetic and copies ran while one was open for 2% of the time, Pallas kernels for 25%

profile of v1, /device:TPU:0, one launch (start us, length us, event | category | flops | bytes accessed | tf_op | source)
XLA Modules:
  0.0 49.5 jit_solution(7512754109357534441)
XLA Ops:
  0.0 0.7 %copy-done.14 = s32[1,4,4]{2,1,0:T(4,128)S(1)} copy-done((s32[1,4,4]{2,1,0:T(4,128)S(1)}, s32[1,4,4]{2,1,0:T(4,128)}, u32[]{:S(2)}) %copy-start.14) | copy-done | bytes 88
  0.7 3.7 %project.1 = (bf16[64,384]{1,0:T(8,128)(2,1)S(1)}, bf16[4096,384]{1,0:T(8,128)(2,1)S(1)}, bf16[4,128,128]{2,1,0:T(8,128)(2,1)S(1)}) custom-call(bf16[2,64,4096]{2,1,0:T(8,128)(2,1)} %bitcast.8, bf16[4096,384]{1,0:T(8,128)(2,1)} %rhs.1, bf16[4,2,2,64,64]{4,3,2,1,0:T(8,128)(2,1)} %bitcast.10, s32[4,4]{1,0:T(4,128)S(1)} %bitcast.6), custom_call_target="tpu_custom_call" | custom-call | flops 805306368 | bytes 4194304 | tf_op jit(solution)/shard_map/project/pallas_call | solution.py:92
  4.4 4.1 %collective-permute-start.1 = (bf16[64,384]{1,0:T(8,128)(2,1)S(1)}, bf16[64,384]{1,0:T(8,128)(2,1)S(1)}, u32[]{:S(2)}, u32[]{:S(2)}) collective-permute-start(bf16[64,384]{1,0:T(8,128)(2,1)S(1)} %get-tuple-element.24.skel), channel_id=1, source_target_pairs={{0,8},{1,9},{2,10},{3,11},{4,12},{5,13},{6,14},{7,15},{8,0},{9,1},... | collective-permute-start | bytes 147464 | tf_op jit(solution)/shard_map/ppermute | solution.py:20
  8.5 2.2 %near_part.4 = (f32[1024,384]{1,0:T(8,128)S(1)}, f32[8,128]{1,0:T(8,128)S(1)}) custom-call(bf16[2,16,256,256]{3,2,1,0:T(8,128)(2,1)} %near.7, bf16[4096,384]{1,0:T(8,128)(2,1)S(1)} %get-tuple-element.25.rhs_keep), custom_call_target="tpu_custom_call" | custom-call | flops 402653184 | bytes 1048576 | tf_op jit(solution)/shard_map/near_part/pallas_call | solution.py:130
  10.7 0.0 copy-start.1
  10.7 1.1 %copy-done.1 = f32[1024,384]{1,0:T(8,128)} copy-done((f32[1024,384]{1,0:T(8,128)}, f32[1024,384]{1,0:T(8,128)S(1)}, u32[]{:S(2)}) %copy-start.1) | copy-done | bytes 1572888
  11.9 0.6 %copy-done.12 = f32[8,128]{1,0:T(8,128)} copy-done((f32[8,128]{1,0:T(8,128)}, f32[8,128]{1,0:T(8,128)S(1)}, u32[]{:S(2)}) %copy-start.12) | copy-done | bytes 4120
  12.5 0.0 collective-permute-done.1.other
  12.5 0.6 %copy-done.20 = bf16[64,384]{1,0:T(8,128)(2,1)} copy-done((bf16[64,384]{1,0:T(8,128)(2,1)}, bf16[64,384]{1,0:T(8,128)(2,1)S(1)}, u32[]{:S(2)}) %copy-start.20) | copy-done | bytes 49176
  13.1 1.2 %level_step.2.skel = bf16[64,384]{1,0:T(8,128)(2,1)S(1)} custom-call(bf16[4,128,128]{2,1,0:T(8,128)(2,1)} %copy-done, bf16[64,384]{1,0:T(8,128)(2,1)} %copy-done.10, bf16[64,384]{1,0:T(8,128)(2,1)} %copy-done.20, f32[8,128]{1,0:T(8,128)} %copy-done.12), custom_call_target="tpu_custom_call" | custom-call | flops 12582912 | bytes 147456 | tf_op jit(solution)/shard_map/level_step/pallas_call | solution.py:198
  14.3 1.6 %collective-permute-start.2 = (bf16[64,384]{1,0:T(8,128)(2,1)S(1)}, bf16[64,384]{1,0:T(8,128)(2,1)S(1)}, u32[]{:S(2)}, u32[]{:S(2)}) collective-permute-start(bf16[64,384]{1,0:T(8,128)(2,1)S(1)} %level_step.2.skel), channel_id=1, source_target_pairs={{0,4},{1,5},{2,6},{3,7},{4,0},{5,1},{6,2},{7,3},{8,12},{9,13},{10,... | collective-permute-start | bytes 147464 | tf_op jit(solution)/shard_map/ppermute | solution.py:20
  15.9 0.8 %slice.3 = bf16[2,128,128]{2,1,0:T(8,128)(2,1)S(1)} slice(bf16[4,128,128]{2,1,0:T(8,128)(2,1)} %copy-done), slice={[2:4], [0:128], [0:128]} | slice | bytes 131072 | tf_op jit(solution)/shard_map/slice | solution.py:312
  16.8 1.5 %collective-permute-start = (bf16[2,128,128]{2,1,0:T(8,128)(2,1)S(1)}, bf16[2,128,128]{2,1,0:T(8,128)(2,1)S(1)}, u32[]{:S(2)}, u32[]{:S(2)}) collective-permute-start(bf16[2,128,128]{2,1,0:T(8,128)(2,1)S(1)} %slice.3), channel_id=1, source_target_pairs={{0,2},{1,3},{2,0},{3,1},{4,6},{5,7},{6,4},{7,5},{8,10},{9,11},{10,... | collective-permute-start | bytes 196616 | tf_op jit(solution)/shard_map/ppermute | solution.py:20
  18.3 2.2 %near_part.5 = (f32[1024,384]{1,0:T(8,128)S(1)}, f32[8,128]{1,0:T(8,128)S(1)}) custom-call(bf16[2,16,256,256]{3,2,1,0:T(8,128)(2,1)} %near.7, bf16[4096,384]{1,0:T(8,128)(2,1)S(1)} %get-tuple-element.25.rhs_keep), custom_call_target="tpu_custom_call" | custom-call | flops 402653184 | bytes 1048576 | tf_op jit(solution)/shard_map/near_part/pallas_call | solution.py:130
  20.5 1.2 %copy-done.3 = f32[1024,384]{1,0:T(8,128)} copy-done((f32[1024,384]{1,0:T(8,128)}, f32[1024,384]{1,0:T(8,128)S(1)}, u32[]{:S(2)}) %copy-start.3) | copy-done | bytes 1572888
  21.7 0.6 %copy-done.13 = f32[8,128]{1,0:T(8,128)} copy-done((f32[8,128]{1,0:T(8,128)}, f32[8,128]{1,0:T(8,128)S(1)}, u32[]{:S(2)}) %copy-start.13) | copy-done | bytes 4120
  22.3 0.0 collective-permute-done.2.other
  22.3 0.6 %copy-done.19 = bf16[64,384]{1,0:T(8,128)(2,1)} copy-done((bf16[64,384]{1,0:T(8,128)(2,1)}, bf16[64,384]{1,0:T(8,128)(2,1)S(1)}, u32[]{:S(2)}) %copy-start.19) | copy-done | bytes 49176
  22.9 1.2 %level_step.3.own = bf16[64,384]{1,0:T(8,128)(2,1)S(1)} custom-call(bf16[4,128,128]{2,1,0:T(8,128)(2,1)} %copy-done, bf16[64,384]{1,0:T(8,128)(2,1)} %copy-done.9, bf16[64,384]{1,0:T(8,128)(2,1)} %copy-done.19, f32[8,128]{1,0:T(8,128)} %copy-done.13), custom_call_target="tpu_custom_call" | custom-call | flops 12582912 | bytes 147456 | tf_op jit(solution)/shard_map/level_step/pallas_call | solution.py:198
  24.1 0.6 %collective-permute-start.3 = (bf16[64,384]{1,0:T(8,128)(2,1)S(1)}, bf16[64,384]{1,0:T(8,128)(2,1)S(1)}, u32[]{:S(2)}, u32[]{:S(2)}) collective-permute-start(bf16[64,384]{1,0:T(8,128)(2,1)S(1)} %level_step.3.own), channel_id=1, source_target_pairs={{0,2},{1,3},{2,0},{3,1},{4,6},{5,7},{6,4},{7,5},{8,10},{9,11},{10,... | collective-permute-start | bytes 147464 | tf_op jit(solution)/shard_map/ppermute | solution.py:20
  24.7 2.2 %near_part.6 = (f32[1024,384]{1,0:T(8,128)S(1)}, f32[8,128]{1,0:T(8,128)S(1)}) custom-call(bf16[2,16,256,256]{3,2,1,0:T(8,128)(2,1)} %near.7, bf16[4096,384]{1,0:T(8,128)(2,1)S(1)} %get-tuple-element.25.rhs_keep), custom_call_target="tpu_custom_call" | custom-call | flops 402653184 | bytes 1048576 | tf_op jit(solution)/shard_map/near_part/pallas_call | solution.py:130
  27.0 1.1 %copy-done.5 = f32[1024,384]{1,0:T(8,128)} copy-done((f32[1024,384]{1,0:T(8,128)}, f32[1024,384]{1,0:T(8,128)S(1)}, u32[]{:S(2)}) %copy-start.5) | copy-done | bytes 1572888
  28.1 0.6 %copy-done.11 = f32[8,128]{1,0:T(8,128)} copy-done((f32[8,128]{1,0:T(8,128)}, f32[8,128]{1,0:T(8,128)S(1)}, u32[]{:S(2)}) %copy-start.11) | copy-done | bytes 4120
  28.7 0.0 collective-permute-done.mix_other
  28.7 0.0 collective-permute-done.3.far
  28.7 0.6 %copy-done.16 = bf16[2,128,128]{2,1,0:T(8,128)(2,1)} copy-done((bf16[2,128,128]{2,1,0:T(8,128)(2,1)}, bf16[2,128,128]{2,1,0:T(8,128)(2,1)S(1)}, u32[]{:S(2)}) %copy-start.16) | copy-done | bytes 65560
  29.3 0.0 copy-done.18
  29.3 1.2 %fork_step.1.own = bf16[128,384]{1,0:T(8,128)(2,1)S(1)} custom-call(bf16[4,128,128]{2,1,0:T(8,128)(2,1)} %copy-done, bf16[2,128,128]{2,1,0:T(8,128)(2,1)} %copy-done.16, bf16[64,384]{1,0:T(8,128)(2,1)} %copy-done.8, bf16[64,384]{1,0:T(8,128)(2,1)} %copy-done.18, f32[8,128]{1,0:T(8,128)} %copy-done.11), custom_call_target="tpu_custom_call" | custom-call | flops 25165824 | bytes 196608 | tf_op jit(solution)/shard_map/fork_step/pallas_call | solution.py:217
  30.6 0.1 collective-permute-start.4
  30.7 1.3 %collective-permute-done.4.far = bf16[128,384]{1,0:T(8,128)(2,1)S(1)} collective-permute-done((bf16[128,384]{1,0:T(8,128)(2,1)S(1)}, bf16[128,384]{1,0:T(8,128)(2,1)S(1)}, u32[]{:S(2)}, u32[]{:S(2)}) %collective-permute-start.4) | collective-permute-done | bytes 98336 | tf_op jit(solution)/shard_map/ppermute | solution.py:20
  32.0 0.7 %copy-done.17 = bf16[128,384]{1,0:T(8,128)(2,1)} copy-done((bf16[128,384]{1,0:T(8,128)(2,1)}, bf16[128,384]{1,0:T(8,128)(2,1)S(1)}, u32[]{:S(2)}) %copy-start.17) | copy-done | bytes 98328
  32.6 1.3 %twin_step.1.refs_0_ = bf16[128,384]{1,0:T(8,128)(2,1)S(1)} custom-call(bf16[4,128,128]{2,1,0:T(8,128)(2,1)} %copy-done, bf16[2,128,128]{2,1,0:T(8,128)(2,1)} %copy-done.16, bf16[128,384]{1,0:T(8,128)(2,1)} %copy-done.7, bf16[128,384]{1,0:T(8,128)(2,1)} %copy-done.17), custom_call_target="tpu_custom_call" | custom-call | flops 50331648 | bytes 393216 | tf_op jit(solution)/shard_map/twin_step/pallas_call | solution.py:236
  34.0 0.5 %collective-permute-start.8 = (bf16[128,384]{1,0:T(8,128)(2,1)S(1)}, bf16[128,384]{1,0:T(8,128)(2,1)S(1)}, u32[]{:S(2)}, u32[]{:S(2)}) collective-permute-start(bf16[128,384]{1,0:T(8,128)(2,1)S(1)} %twin_step.1.refs_0_), channel_id=1, source_target_pairs={{0,4},{1,5},{2,6},{3,7},{4,0},{5,1},{6,2},{7,3},{8,12},{9,13},{10,... | collective-permute-start | bytes 294920 | tf_op jit(solution)/shard_map/ppermute | solution.py:20
  34.5 1.0 %collective-permute-start.7 = (bf16[128,384]{1,0:T(8,128)(2,1)S(1)}, bf16[128,384]{1,0:T(8,128)(2,1)S(1)}, u32[]{:S(2)}, u32[]{:S(2)}) collective-permute-start(bf16[128,384]{1,0:T(8,128)(2,1)S(1)} %twin_step.1.refs_0_), channel_id=1, source_target_pairs={{0,8},{1,9},{2,10},{3,11},{4,12},{5,13},{6,14},{7,15},{8,0},{9,1},... | collective-permute-start | bytes 294920 | tf_op jit(solution)/shard_map/ppermute | solution.py:20
  35.5 2.9 %collective-permute-start.6 = (bf16[128,384]{1,0:T(8,128)(2,1)S(1)}, bf16[128,384]{1,0:T(8,128)(2,1)S(1)}, u32[]{:S(2)}, u32[]{:S(2)}) collective-permute-start(bf16[128,384]{1,0:T(8,128)(2,1)S(1)} %twin_step.1.refs_0_), channel_id=1, source_target_pairs={{0,12},{1,13},{2,14},{3,15},{4,8},{5,9},{6,10},{7,11},{8,4},{9,5},... | collective-permute-start | bytes 294920 | tf_op jit(solution)/shard_map/ppermute | solution.py:20
  38.4 2.4 %near_part.7 = (f32[1024,384]{1,0:T(8,128)S(1)}, f32[8,128]{1,0:T(8,128)S(1)}) custom-call(bf16[2,16,256,256]{3,2,1,0:T(8,128)(2,1)} %near.7, bf16[4096,384]{1,0:T(8,128)(2,1)S(1)} %get-tuple-element.25.rhs_keep), custom_call_target="tpu_custom_call" | custom-call | flops 402653184 | bytes 1048576 | tf_op jit(solution)/shard_map/near_part/pallas_call | solution.py:130
  40.8 2.3 %prepare.1 = (bf16[4096,128]{1,0:T(8,128)(2,1)S(1)}, bf16[4,128,256]{2,1,0:T(8,128)(2,1)S(1)}) custom-call(bf16[2,64,4096]{2,1,0:T(8,128)(2,1)} %bitcast.7, bf16[16,2,64,64]{3,2,1,0:T(8,128)(2,1)} %bitcast.9, s32[1,16]{1,0:T(1,128)S(1)} %copy-done.15, s32[1]{0:T(128)} %bitcast.5.here, f32[8,128]{1,0:T(8,128)S(1)} %get-tuple-element.29.token), custom_call_target="tpu_custom_call" | custom-call | flops 524288 | bytes 2621440 | tf_op jit(solution)/shard_map/prepare/pallas_call | solution.py:172
  43.1 0.1 collective-permute-start.5
  43.2 0.0 collective-permute-done.8.refs_6_
  43.2 2.0 %collective-permute-done.7.refs_4_ = bf16[128,384]{1,0:T(8,128)(2,1)S(1)} collective-permute-done((bf16[128,384]{1,0:T(8,128)(2,1)S(1)}, bf16[128,384]{1,0:T(8,128)(2,1)S(1)}, u32[]{:S(2)}, u32[]{:S(2)}) %collective-permute-start.7) | collective-permute-done | bytes 98336 | tf_op jit(solution)/shard_map/ppermute | solution.py:20
  45.2 0.0 collective-permute-done.6.refs_2_
  45.2 0.0 collective-permute-start.9
  45.2 0.5 %collective-permute-start.10 = (bf16[128,384]{1,0:T(8,128)(2,1)S(1)}, bf16[128,384]{1,0:T(8,128)(2,1)S(1)}, u32[]{:S(2)}, u32[]{:S(2)}) collective-permute-start(bf16[128,384]{1,0:T(8,128)(2,1)S(1)} %collective-permute-done.7.refs_4_), channel_id=1, source_target_pairs={{0,1},{1,0},{2,3},{3,2},{4,5},{5,4},{6,7},{7,6},{8,9},{9,8},{10,11... | collective-permute-start | bytes 294920 | tf_op jit(solution)/shard_map/ppermute | solution.py:20
  45.7 0.0 collective-permute-start.11
  45.7 0.8 %collective-permute-done.9.refs_3_ = bf16[128,384]{1,0:T(8,128)(2,1)S(1)} collective-permute-done((bf16[128,384]{1,0:T(8,128)(2,1)S(1)}, bf16[128,384]{1,0:T(8,128)(2,1)S(1)}, u32[]{:S(2)}, u32[]{:S(2)}) %collective-permute-start.9) | collective-permute-done | bytes 98336 | tf_op jit(solution)/shard_map/ppermute | solution.py:20
  46.5 0.2 collective-permute-done.10.refs_5_
  46.7 0.4 collective-permute-done.11.refs_7_
  47.0 2.5 %finish.1 = bf16[4096,384]{1,0:T(8,128)(2,1)} custom-call(bf16[128,384]{1,0:T(8,128)(2,1)S(1)} %twin_step.1.refs_0_, bf16[128,384]{1,0:T(8,128)(2,1)S(1)} %collective-permute-done.5.refs_1_, bf16[128,384]{1,0:T(8,128)(2,1)S(1)} %collective-permute-done.6.refs_2_, bf16[128,384]{1,0:T(8,128)(2,1)S(1)} %collective-permute-done.9.refs_3_, ...), custom_call_target="tpu_custom_call" | custom-call | flops 402653184 | bytes 9437184 | tf_op jit(solution)/shard_map/finish/pallas_call | solution.py:278
  (30 shorter events, 0.1 us)
Async XLA Ops:
  0.0 0.7 %copy-start.14 = (s32[1,4,4]{2,1,0:T(4,128)S(1)}, s32[1,4,4]{2,1,0:T(4,128)}, u32[]{:S(2)}) copy-start(s32[1,4,4]{2,1,0:T(4,128)} %param.14) | copy-start | bytes 196
  4.4 6.4 %copy-start = (bf16[4,128,128]{2,1,0:T(8,128)(2,1)}, bf16[4,128,128]{2,1,0:T(8,128)(2,1)S(1)}, u32[]{:S(2)}) copy-start(bf16[4,128,128]{2,1,0:T(8,128)(2,1)S(1)} %get-tuple-element.23.mixers.mix) | copy-start | bytes 393220
  4.4 6.4 %copy-start.10 = (bf16[64,384]{1,0:T(8,128)(2,1)}, bf16[64,384]{1,0:T(8,128)(2,1)S(1)}, u32[]{:S(2)}) copy-start(bf16[64,384]{1,0:T(8,128)(2,1)S(1)} %get-tuple-element.24.skel) | copy-start | bytes 147460
  4.4 8.1 %collective-permute-start.1 = (bf16[64,384]{1,0:T(8,128)(2,1)S(1)}, bf16[64,384]{1,0:T(8,128)(2,1)S(1)}, u32[]{:S(2)}, u32[]{:S(2)}) collective-permute-start(bf16[64,384]{1,0:T(8,128)(2,1)S(1)} %get-tuple-element.24.skel), channel_id=1, source_target_pairs={{0,8},{1,9},{2,10},{3,11},{4,12},{5,13},{6,14},{7,15},{8,0},{9,1},... | collective-permute-start | bytes 147464 | tf_op jit(solution)/shard_map/ppermute | solution.py:20
  10.7 1.1 %copy-start.1 = (f32[1024,384]{1,0:T(8,128)}, f32[1024,384]{1,0:T(8,128)S(1)}, u32[]{:S(2)}) copy-start(f32[1024,384]{1,0:T(8,128)S(1)} %get-tuple-element.35.refs_8_) | copy-start | bytes 4718596
  11.9 0.6 %copy-start.12 = (f32[8,128]{1,0:T(8,128)}, f32[8,128]{1,0:T(8,128)S(1)}, u32[]{:S(2)}) copy-start(f32[8,128]{1,0:T(8,128)S(1)} %get-tuple-element.26.token) | copy-start | bytes 12292
  12.5 0.6 %copy-start.20 = (bf16[64,384]{1,0:T(8,128)(2,1)}, bf16[64,384]{1,0:T(8,128)(2,1)S(1)}, u32[]{:S(2)}) copy-start(bf16[64,384]{1,0:T(8,128)(2,1)S(1)} %collective-permute-done.1.other) | copy-start | bytes 147460
  14.3 6.2 %copy-start.9 = (bf16[64,384]{1,0:T(8,128)(2,1)}, bf16[64,384]{1,0:T(8,128)(2,1)S(1)}, u32[]{:S(2)}) copy-start(bf16[64,384]{1,0:T(8,128)(2,1)S(1)} %level_step.2.skel) | copy-start | bytes 147460
  14.3 8.0 %collective-permute-start.2 = (bf16[64,384]{1,0:T(8,128)(2,1)S(1)}, bf16[64,384]{1,0:T(8,128)(2,1)S(1)}, u32[]{:S(2)}, u32[]{:S(2)}) collective-permute-start(bf16[64,384]{1,0:T(8,128)(2,1)S(1)} %level_step.2.skel), channel_id=1, source_target_pairs={{0,4},{1,5},{2,6},{3,7},{4,0},{5,1},{6,2},{7,3},{8,12},{9,13},{10,... | collective-permute-start | bytes 147464 | tf_op jit(solution)/shard_map/ppermute | solution.py:20
  16.8 11.9 %collective-permute-start = (bf16[2,128,128]{2,1,0:T(8,128)(2,1)S(1)}, bf16[2,128,128]{2,1,0:T(8,128)(2,1)S(1)}, u32[]{:S(2)}, u32[]{:S(2)}) collective-permute-start(bf16[2,128,128]{2,1,0:T(8,128)(2,1)S(1)} %slice.3), channel_id=1, source_target_pairs={{0,2},{1,3},{2,0},{3,1},{4,6},{5,7},{6,4},{7,5},{8,10},{9,11},{10,... | collective-permute-start | bytes 196616 | tf_op jit(solution)/shard_map/ppermute | solution.py:20
  20.5 1.2 %copy-start.3 = (f32[1024,384]{1,0:T(8,128)}, f32[1024,384]{1,0:T(8,128)S(1)}, u32[]{:S(2)}) copy-start(f32[1024,384]{1,0:T(8,128)S(1)} %get-tuple-element.36.refs_9_) | copy-start | bytes 4718596
  21.7 0.6 %copy-start.13 = (f32[8,128]{1,0:T(8,128)}, f32[8,128]{1,0:T(8,128)S(1)}, u32[]{:S(2)}) copy-start(f32[8,128]{1,0:T(8,128)S(1)} %get-tuple-element.27.token) | copy-start | bytes 12292
  22.3 0.6 %copy-start.19 = (bf16[64,384]{1,0:T(8,128)(2,1)}, bf16[64,384]{1,0:T(8,128)(2,1)S(1)}, u32[]{:S(2)}) copy-start(bf16[64,384]{1,0:T(8,128)(2,1)S(1)} %collective-permute-done.2.other) | copy-start | bytes 147460
  24.1 2.8 %copy-start.8 = (bf16[64,384]{1,0:T(8,128)(2,1)}, bf16[64,384]{1,0:T(8,128)(2,1)S(1)}, u32[]{:S(2)}) copy-start(bf16[64,384]{1,0:T(8,128)(2,1)S(1)} %level_step.3.own) | copy-start | bytes 147460
  24.1 4.6 %collective-permute-start.3 = (bf16[64,384]{1,0:T(8,128)(2,1)S(1)}, bf16[64,384]{1,0:T(8,128)(2,1)S(1)}, u32[]{:S(2)}, u32[]{:S(2)}) collective-permute-start(bf16[64,384]{1,0:T(8,128)(2,1)S(1)} %level_step.3.own), channel_id=1, source_target_pairs={{0,2},{1,3},{2,0},{3,1},{4,6},{5,7},{6,4},{7,5},{8,10},{9,11},{10,... | collective-permute-start | bytes 147464 | tf_op jit(solution)/shard_map/ppermute | solution.py:20
  26.9 1.2 %copy-start.5 = (f32[1024,384]{1,0:T(8,128)}, f32[1024,384]{1,0:T(8,128)S(1)}, u32[]{:S(2)}) copy-start(f32[1024,384]{1,0:T(8,128)S(1)} %get-tuple-element.37.refs_10_) | copy-start | bytes 4718596
  28.1 0.6 %copy-start.11 = (f32[8,128]{1,0:T(8,128)}, f32[8,128]{1,0:T(8,128)S(1)}, u32[]{:S(2)}) copy-start(f32[8,128]{1,0:T(8,128)S(1)} %get-tuple-element.28.token) | copy-start | bytes 12292
  28.7 0.6 %copy-start.16 = (bf16[2,128,128]{2,1,0:T(8,128)(2,1)}, bf16[2,128,128]{2,1,0:T(8,128)(2,1)S(1)}, u32[]{:S(2)}) copy-start(bf16[2,128,128]{2,1,0:T(8,128)(2,1)S(1)} %collective-permute-done.mix_other) | copy-start | bytes 196612
  28.7 0.6 %copy-start.18 = (bf16[64,384]{1,0:T(8,128)(2,1)}, bf16[64,384]{1,0:T(8,128)(2,1)S(1)}, u32[]{:S(2)}) copy-start(bf16[64,384]{1,0:T(8,128)(2,1)S(1)} %collective-permute-done.3.far) | copy-start | bytes 147460
  30.6 1.4 %copy-start.7 = (bf16[128,384]{1,0:T(8,128)(2,1)}, bf16[128,384]{1,0:T(8,128)(2,1)S(1)}, u32[]{:S(2)}) copy-start(bf16[128,384]{1,0:T(8,128)(2,1)S(1)} %fork_step.1.own) | copy-start | bytes 294916
  30.6 1.4 %collective-permute-start.4 = (bf16[128,384]{1,0:T(8,128)(2,1)S(1)}, bf16[128,384]{1,0:T(8,128)(2,1)S(1)}, u32[]{:S(2)}, u32[]{:S(2)}) collective-permute-start(bf16[128,384]{1,0:T(8,128)(2,1)S(1)} %fork_step.1.own), channel_id=1, source_target_pairs={{0,1},{1,0},{2,3},{3,2},{4,5},{5,4},{6,7},{7,6},{8,9},{9,8},{10,11... | collective-permute-start | bytes 294920 | tf_op jit(solution)/shard_map/ppermute | solution.py:20
  32.0 0.7 %copy-start.17 = (bf16[128,384]{1,0:T(8,128)(2,1)}, bf16[128,384]{1,0:T(8,128)(2,1)S(1)}, u32[]{:S(2)}) copy-start(bf16[128,384]{1,0:T(8,128)(2,1)S(1)} %collective-permute-done.4.far) | copy-start | bytes 294916
  34.0 9.2 %collective-permute-start.8 = (bf16[128,384]{1,0:T(8,128)(2,1)S(1)}, bf16[128,384]{1,0:T(8,128)(2,1)S(1)}, u32[]{:S(2)}, u32[]{:S(2)}) collective-permute-start(bf16[128,384]{1,0:T(8,128)(2,1)S(1)} %twin_step.1.refs_0_), channel_id=1, source_target_pairs={{0,4},{1,5},{2,6},{3,7},{4,0},{5,1},{6,2},{7,3},{8,12},{9,13},{10,... | collective-permute-start | bytes 294920 | tf_op jit(solution)/shard_map/ppermute | solution.py:20
  34.5 10.7 %collective-permute-start.7 = (bf16[128,384]{1,0:T(8,128)(2,1)S(1)}, bf16[128,384]{1,0:T(8,128)(2,1)S(1)}, u32[]{:S(2)}, u32[]{:S(2)}) collective-permute-start(bf16[128,384]{1,0:T(8,128)(2,1)S(1)} %twin_step.1.refs_0_), channel_id=1, source_target_pairs={{0,8},{1,9},{2,10},{3,11},{4,12},{5,13},{6,14},{7,15},{8,0},{9,1},... | collective-permute-start | bytes 294920 | tf_op jit(solution)/shard_map/ppermute | solution.py:20
  35.5 9.7 %collective-permute-start.6 = (bf16[128,384]{1,0:T(8,128)(2,1)S(1)}, bf16[128,384]{1,0:T(8,128)(2,1)S(1)}, u32[]{:S(2)}, u32[]{:S(2)}) collective-permute-start(bf16[128,384]{1,0:T(8,128)(2,1)S(1)} %twin_step.1.refs_0_), channel_id=1, source_target_pairs={{0,12},{1,13},{2,14},{3,15},{4,8},{5,9},{6,10},{7,11},{8,4},{9,5},... | collective-permute-start | bytes 294920 | tf_op jit(solution)/shard_map/ppermute | solution.py:20
  38.4 2.4 %copy-start.15 = (s32[1,16]{1,0:T(1,128)S(1)}, s32[1,16]{1,0:T(1,128)}, u32[]{:S(2)}) copy-start(s32[1,16]{1,0:T(1,128)} %order.1) | copy-start | bytes 196
  38.4 8.6 %copy-start.2 = (f32[1024,384]{1,0:T(8,128)S(1)}, f32[1024,384]{1,0:T(8,128)}, u32[]{:S(2)}) copy-start(f32[1024,384]{1,0:T(8,128)} %copy-done.1) | copy-start | bytes 4718596
  38.4 8.6 %copy-start.4 = (f32[1024,384]{1,0:T(8,128)S(1)}, f32[1024,384]{1,0:T(8,128)}, u32[]{:S(2)}) copy-start(f32[1024,384]{1,0:T(8,128)} %copy-done.3) | copy-start | bytes 4718596
  38.4 8.6 %copy-start.6 = (f32[1024,384]{1,0:T(8,128)S(1)}, f32[1024,384]{1,0:T(8,128)}, u32[]{:S(2)}) copy-start(f32[1024,384]{1,0:T(8,128)} %copy-done.5) | copy-start | bytes 4718596
  43.1 2.6 %collective-permute-start.5 = (bf16[128,384]{1,0:T(8,128)(2,1)S(1)}, bf16[128,384]{1,0:T(8,128)(2,1)S(1)}, u32[]{:S(2)}, u32[]{:S(2)}) collective-permute-start(bf16[128,384]{1,0:T(8,128)(2,1)S(1)} %twin_step.1.refs_0_), channel_id=1, source_target_pairs={{0,1},{1,0},{2,3},{3,2},{4,5},{5,4},{6,7},{7,6},{8,9},{9,8},{10,11... | collective-permute-start | bytes 294920 | tf_op jit(solution)/shard_map/ppermute | solution.py:20
  45.2 1.3 %collective-permute-start.9 = (bf16[128,384]{1,0:T(8,128)(2,1)S(1)}, bf16[128,384]{1,0:T(8,128)(2,1)S(1)}, u32[]{:S(2)}, u32[]{:S(2)}) collective-permute-start(bf16[128,384]{1,0:T(8,128)(2,1)S(1)} %collective-permute-done.6.refs_2_), channel_id=1, source_target_pairs={{0,1},{1,0},{2,3},{3,2},{4,5},{5,4},{6,7},{7,6},{8,9},{9,8},{10,11... | collective-permute-start | bytes 294920 | tf_op jit(solution)/shard_map/ppermute | solution.py:20
  45.2 1.5 %collective-permute-start.10 = (bf16[128,384]{1,0:T(8,128)(2,1)S(1)}, bf16[128,384]{1,0:T(8,128)(2,1)S(1)}, u32[]{:S(2)}, u32[]{:S(2)}) collective-permute-start(bf16[128,384]{1,0:T(8,128)(2,1)S(1)} %collective-permute-done.7.refs_4_), channel_id=1, source_target_pairs={{0,1},{1,0},{2,3},{3,2},{4,5},{5,4},{6,7},{7,6},{8,9},{9,8},{10,11... | collective-permute-start | bytes 294920 | tf_op jit(solution)/shard_map/ppermute | solution.py:20
  45.7 1.3 %collective-permute-start.11 = (bf16[128,384]{1,0:T(8,128)(2,1)S(1)}, bf16[128,384]{1,0:T(8,128)(2,1)S(1)}, u32[]{:S(2)}, u32[]{:S(2)}) collective-permute-start(bf16[128,384]{1,0:T(8,128)(2,1)S(1)} %collective-permute-done.8.refs_6_), channel_id=1, source_target_pairs={{0,1},{1,0},{2,3},{3,2},{4,5},{5,4},{6,7},{7,6},{8,9},{9,8},{10,11... | collective-permute-start | bytes 294920 | tf_op jit(solution)/shard_map/ppermute | solution.py:20

commit v2 on v1

v2 whole, which is shorter than its diff:
```python
import functools

import jax
import jax.numpy as jnp
from jax import lax
from jax.experimental import pallas as pl
from jax.experimental.pallas import tpu as pltpu
from jax.sharding import PartitionSpec as P

BF = jnp.bfloat16
F32 = jnp.float32
VMEM = pl.BlockSpec(memory_space=pltpu.VMEM)
SMEM = pl.BlockSpec(memory_space=pltpu.SMEM)
ANY = pl.BlockSpec(memory_space=pl.ANY)
HBM = pl.BlockSpec(memory_space=pltpu.HBM)


def partner(array, apart):
    count = lax.axis_size("leaf")
    return lax.ppermute(array, "leaf", [(i, i ^ apart) for i in range(count)])


def in_hbm(array):
    return pltpu.with_memory_space_constraint(array, pltpu.HBM)


def turned(block):
    half = block.shape[1] // 2
    return jnp.concatenate([-block[:, half:], block[:, :half]], axis=1)


def combined(stacked):
    rank = stacked.shape[0] // 2
    return stacked[:rank] + turned(stacked[rank:])


def dot(a, b):
    return jnp.dot(a, b, preferred_element_type=F32)


def params(mib):
    return pltpu.CompilerParams(vmem_limit_bytes=mib * 2**20)


def cost(flops, moved):
    return pl.CostEstimate(flops=flops, bytes_accessed=moved, transcendentals=0)


def project_kernel(cuts, left, rhs, skel, rhs_keep, left_buf, sems):
    rank = left.shape[1]
    copies = []
    start = 0
    for c, depth in enumerate(cuts):
        span = pl.ds(start, depth)
        copies.append((
            span,
            pltpu.make_async_copy(left.at[:, :, span], left_buf.at[:, :, span], sems.at[2 * c]),
            pltpu.make_async_copy(rhs.at[span], rhs_keep.at[span], sems.at[2 * c + 1]),
        ))
        start += depth
    for _, one, two in copies:
        one.start()
        two.start()
    total = None
    for span, one, two in copies:
        one.wait()
        two.wait()
        term = dot(left_buf[:, :, span].reshape(2 * rank, span.size), rhs_keep[span, :])
        total = term if total is None else total + term
    skel[...] = combined(total).astype(BF)


def project(left_t, rhs):
    rank = left_t.shape[1]
    rows = rhs.shape[0]
    cuts = (rows // 2, rows // 4, rows // 4)
    return pl.pallas_call(
        functools.partial(project_kernel, cuts),
        out_shape=(pltpu.VMEM((rank, rhs.shape[1]), BF), pltpu.VMEM(rhs.shape, BF)),
        in_specs=[HBM, HBM],
        out_specs=(VMEM, VMEM),
        scratch_shapes=[pltpu.VMEM(left_t.shape, BF), pltpu.SemaphoreType.DMA((2 * len(cuts),))],
        compiler_params=params(4),
        cost_estimate=cost(4 * left_t.size * rhs.shape[1], 2 * (left_t.size + rhs.size)),
        name="project",
    )(left_t, rhs)


def mixers_kernel(factors, pattern, after, first, rest, fac_buf, pat_buf, sems):
    levels = factors.shape[0]
    blocks = pattern.shape[1]
    rank = factors.shape[3]
    one = pltpu.make_async_copy(factors, fac_buf, sems.at[0])
    two = pltpu.make_async_copy(pattern, pat_buf, sems.at[1])
    one.start()
    two.start()
    one.wait()
    two.wait()
    high = rank // blocks
    for level in range(levels):
        out, at = (first, 0) if level == 0 else (rest, level - 1)
        for part in range(2):
            own = fac_buf[level, 0, part]
            cross = fac_buf[level, 1, part].astype(F32)
            pieces = [cross[r * high:(r + 1) * high, :] * pat_buf[level, r].astype(F32) for r in range(blocks)]
            masked = jnp.concatenate(pieces, axis=0).astype(BF)
            out[at, pl.ds(part * rank, rank), :] = jnp.concatenate([own, masked], axis=1)


def make_mixers(factors, pattern, after):
    levels = factors.shape[0]
    rank = factors.shape[3]
    return pl.pallas_call(
        mixers_kernel,
        out_shape=(
            pltpu.VMEM((1, 2 * rank, 2 * rank), BF),
            pltpu.VMEM((levels - 1, 2 * rank, 2 * rank), BF),
        ),
        in_specs=[HBM, HBM, ANY],
        out_specs=(VMEM, VMEM),
        scratch_shapes=[
            pltpu.VMEM(factors.shape, BF),
            pltpu.SMEM(pattern.shape, jnp.int32),
            pltpu.SemaphoreType.DMA((2,)),
        ],
        compiler_params=params(2),
        cost_estimate=cost(factors.size, 4 * factors.size),
        name="mixers",
    )(factors, pattern, after)


def behind_kernel(members, groups, near, rhs_keep, right, coupling, order, here, after,
                  out, right_rows, table, buf, right_buf, couple_buf, slot, sems):
    rank = right.shape[1]
    rows = right.shape[2]
    boxes, width = near.shape[1], near.shape[2]
    group = coupling.shape[0]
    each = boxes // groups
    copies = []
    for g in range(groups):
        span = pl.ds(g * each, each)
        copies.append(pltpu.make_async_copy(near.at[:, span], buf.at[:, span], sems.at[g]))
    couple_copy = pltpu.make_async_copy(coupling, couple_buf, sems.at[groups])
    right_copy = pltpu.make_async_copy(right, right_buf, sems.at[groups + 1])
    right_copy.start()
    couple_copy.start()
    for copy in copies:
        copy.start()
    for j in range(group):
        slot[order[0, j] ^ here[0]] = j
    right_copy.wait()
    depth = rows // 8
    for c in range(8):
        span = pl.ds(c * depth, depth)
        right_rows[span, :] = right_buf[:, :, span].reshape(2 * rank, depth).T
    couple_copy.wait()
    per = len(members[0])
    for row in range(len(members)):
        for part in range(2):
            pieces = [couple_buf[slot[members[row][i]], part] for i in range(per)]
            table[row, pl.ds(part * rank, rank), :] = jnp.concatenate(pieces, axis=1)
    for g in range(groups):
        copies[g].wait()
        for b in range(g * each, (g + 1) * each):
            rows_b = pl.ds(b * width, width)
            block = rhs_keep[rows_b, :]
            out[rows_b, :] = dot(buf[0, b], block) + dot(buf[1, b], turned(block))


def behind(near, rhs_keep, right_t, coupling, order, here, members, after):
    groups = 4
    rank = right_t.shape[1]
    rows = right_t.shape[2]
    width = near.shape[2]
    cols = rhs_keep.shape[1]
    return pl.pallas_call(
        functools.partial(behind_kernel, members, groups),
        out_shape=(
            pltpu.VMEM((rows, cols), F32),
            pltpu.VMEM((rows, 2 * rank), BF),
            pltpu.VMEM((len(members), 2 * rank, len(members[0]) * rank), BF),
        ),
        in_specs=[HBM, VMEM, HBM, HBM, SMEM, SMEM, ANY],
        out_specs=(VMEM, VMEM, VMEM),
        scratch_shapes=[
            pltpu.VMEM(near.shape, BF),
            pltpu.VMEM(right_t.shape, BF),
            pltpu.VMEM(coupling.shape, BF),
            pltpu.SMEM((coupling.shape[0],), jnp.int32),
            pltpu.SemaphoreType.DMA((groups + 2,)),
        ],
        compiler_params=params(10),
        cost_estimate=cost(4 * rows * width * cols, 2 * near.size + 2 * right_t.size + 4 * coupling.size),
        name="behind",
    )(near, rhs_keep, right_t, coupling, order, here, after)


def mixed(matrix, one, two):
    return combined(dot(matrix, jnp.concatenate([one, two], axis=0))).astype(BF)


def level_kernel(level, mixers, skel, other, out):
    out[...] = mixed(mixers[level], skel[...], other[...])


def level_step(level, mixers, skel, other):
    return pl.pallas_call(
        functools.partial(level_kernel, level),
        out_shape=pltpu.VMEM(skel.shape, BF),
        in_specs=[VMEM, VMEM, VMEM],
        out_specs=VMEM,
        compiler_params=params(1),
        cost_estimate=cost(8 * skel.shape[0] * skel.size, 6 * skel.size),
        name="level_step",
    )(mixers, skel, other)


def quad_kernel(mix, mix_y, skel, skel_z, skel_y, skel_zy, out):
    rank = skel.shape[0]
    here = mixed(mix[0], skel[...], skel_z[...])
    there = mixed(mix_y[0], skel_y[...], skel_zy[...])
    out[:rank, :] = mixed(mix[1], here, there)
    out[rank:, :] = mixed(mix_y[1], there, here)


def quad_step(mix, mix_y, skel, skel_z, skel_y, skel_zy):
    rank, cols = skel.shape
    return pl.pallas_call(
        quad_kernel,
        out_shape=pltpu.VMEM((2 * rank, cols), BF),
        in_specs=[VMEM] * 6,
        out_specs=VMEM,
        compiler_params=params(1),
        cost_estimate=cost(32 * rank * skel.size, 12 * skel.size),
        name="quad_step",
    )(mix, mix_y, skel, skel_z, skel_y, skel_zy)


def twin_kernel(mix, mix_y, pair, far, out):
    rank = pair.shape[0] // 2
    out[:rank, :] = mixed(mix[2], pair[:rank, :], far[:rank, :])
    out[rank:, :] = mixed(mix_y[2], pair[rank:, :], far[rank:, :])


def twin_step(mix, mix_y, pair, far):
    return pl.pallas_call(
        twin_kernel,
        out_shape=pltpu.VMEM(pair.shape, BF),
        in_specs=[VMEM] * 4,
        out_specs=VMEM,
        compiler_params=params(1),
        cost_estimate=cost(8 * pair.shape[0] * pair.size, 8 * pair.size),
        name="twin_step",
    )(mix, mix_y, pair, far)


def finish_kernel(n_blocks, chunks, *refs):
    blocks = refs[:n_blocks]
    near, table, right_rows, out, buf, sems = refs[n_blocks:]
    per = table.shape[2] // blocks[0].shape[0]
    total = None
    for row in range(table.shape[0]):
        both = jnp.concatenate([ref[...] for ref in blocks[row * per:(row + 1) * per]], axis=0)
        term = dot(table[row], both)
        total = term if total is None else total + term
    coarse = combined(total).astype(BF)
    weights = jnp.concatenate([coarse, turned(coarse)], axis=0)
    depth = buf.shape[0] // chunks
    copies = []
    for c in range(chunks):
        span = pl.ds(c * depth, depth)
        buf[span, :] = (dot(right_rows[span, :], weights) + near[span, :]).astype(BF)
        copies.append(pltpu.make_async_copy(buf.at[span], out.at[span], sems.at[c]))
        copies[-1].start()
    for copy in copies:
        copy.wait()


def finish(blocks, near, table, right_rows):
    chunks = 8
    rows, cols = near.shape
    return pl.pallas_call(
        functools.partial(finish_kernel, len(blocks), chunks),
        out_shape=jax.ShapeDtypeStruct((rows, cols), BF),
        in_specs=[VMEM] * (len(blocks) + 3),
        out_specs=ANY,
        scratch_shapes=[pltpu.VMEM((rows, cols), BF), pltpu.SemaphoreType.DMA((chunks,))],
        compiler_params=params(8),
        cost_estimate=cost(2 * rows * right_rows.shape[1] * cols, 6 * rows * cols),
        name="finish",
    )(*blocks, near, table, right_rows)


def per_device(rhs, left_basis, right_basis, near_field, factors, coupling, pattern, leaf_order):
    leaves = lax.axis_size("leaf")
    bits = leaves.bit_length() - 1
    levels = factors.shape[1]
    group = leaf_order.shape[1]
    boxes = near_field.shape[1]
    left_t = in_hbm(jnp.swapaxes(left_basis, 1, 2))
    right_t = in_hbm(jnp.swapaxes(right_basis, 1, 2))
    near_field = in_hbm(near_field)
    couple = in_hbm(coupling[0])
    here = (lax.axis_index("leaf") % group).astype(jnp.int32)[None]

    skel, rhs_keep = project(left_t, in_hbm(rhs))
    first, rest = make_mixers(in_hbm(factors[0]), in_hbm(pattern[0]), skel)
    run_behind = functools.partial(behind, near_field, rhs_keep, right_t, couple, leaf_order, here)

    if leaves == group == 16 and levels == 4:
        rest_y = partner(rest, 2)
        skel = level_step(0, first, skel, partner(skel, 8))
        pair = quad_step(rest, rest_y, skel, partner(skel, 4), partner(skel, 2), partner(skel, 6))
        pair = twin_step(rest, rest_y, pair, partner(pair, 1))
        far = [partner(pair, 4 * k) for k in (3, 2, 1)]
        members = tuple((4 * k, 4 * k + 2, 4 * k + 1, 4 * k + 3) for k in (0, 3, 2, 1))
        near, right_rows, table = run_behind(members, pair)
        blocks = [pair, partner(pair, 1)]
        for block in far:
            block, table = lax.optimization_barrier((block, table))
            blocks += [block, partner(block, 1)]
    else:
        for level in range(levels):
            matrix, at = (first, 0) if level == 0 else (rest, level - 1)
            skel = level_step(at, matrix, skel, partner(skel, 1 << (bits - 1 - level)))
        blocks = [skel]
        names = [0]
        for bit in reversed(range(group.bit_length() - 1)):
            other = partner(jnp.stack(blocks), 1 << bit)
            blocks = blocks + [other[i] for i in range(len(blocks))]
            names = names + [n ^ (1 << bit) for n in names]
        members = tuple(tuple(names[i:i + 4]) for i in range(0, group, 4))
        near, right_rows, table = run_behind(members, skel)
    return finish(blocks, near, table, right_rows)


def solution(mesh):
    both = ("parts", "leaf")
    in_specs = (
        P(both, None),
        P(None, both, None),
        P(None, both, None),
        P(None, both, None, None),
        P(both, None, None, None, None, None),
        P(both, None, None, None, None),
        P(both, None, None),
        P(both, None),
    )
    return jax.shard_map(
        per_device, mesh=mesh, in_specs=in_specs, out_specs=P(both, None), check_vma=False
    )
```

time: 49.8 us -> 35.1 us (0.70)
  local copies, waits for them, and re-layouts: 9.33 us -> 0.01 us
  Pallas kernels: 22.4 us -> 13.2 us
  waiting for transfers between devices: 4.62 us -> 7.36 us
  starting transfers between devices: 12.9 us -> 14.3 us
    unnamed x42 -> x2, local copies, waits for them, and re-layouts: 8.48 us -> 0.01 us
    pallas_call x9 -> x6, Pallas kernels: 20 us -> 13 us  [the longest x1 5.72 us: behind(): pl.pallas_call(functools.partial(behind_kernel, members, groups), out_sha...]
    ppermute x12 -> x13, waiting for transfers between devices: 4.62 us -> 7.36 us  [partner(): return lax.ppermute(array, 'leaf', [(i, i ^ apart) for i in range(count)])]
    pallas_call x2 -> x1, Pallas kernels: 2.38 us -> 0.25 us  [level_step(): pl.pallas_call(functools.partial(level_kernel, level), out_shape=pltpu.VM...]
    ppermute x12 -> x13, starting transfers between devices: 12.9 us -> 14.3 us  [partner(): return lax.ppermute(array, 'leaf', [(i, i ^ apart) for i in range(count)])]
    slice x1 -> x0, local copies, waits for them, and re-layouts: 0.84 us -> none  [per_device(): mixers_other = partner(mixers[2:], 2)]
  transfers between devices with their start and end apart: 12 -> 13, of which waited for: 5 -> 8; matrix products, arithmetic and copies ran while one was open for 2% -> 0% of each run, Pallas kernels for 25% -> 20%
where the time goes in v2:
time: 35.1 us; the launch traced here: 35 us
  starting transfers between devices  14.3 us (41%)
  Pallas kernels  13.2 us (38%)
  waiting for transfers between devices  7.36 us (21%)
    ppermute x13, starting transfers between devices, partner(): return lax.ppermute(array, 'leaf', [(i, i ^ apart) for i in range(count)])  14.3 us
    ppermute x13, waiting for transfers between devices, partner(): return lax.ppermute(array, 'leaf', [(i, i ^ apart) for i in range(count)])  7.36 us
    pallas_call x1, Pallas kernels, behind(): pl.pallas_call(functools.partial(behind_kernel, members, groups), out_sha...  5.72 us
    pallas_call x1, Pallas kernels, project(): pl.pallas_call(functools.partial(project_kernel, cuts), out_shape=(pltpu....  2.84 us
    pallas_call x1, Pallas kernels, finish(): pl.pallas_call(functools.partial(finish_kernel, len(blocks), chunks), out...  2.44 us
    pallas_call x1, Pallas kernels, make_mixers(): pl.pallas_call(mixers_kernel, out_shape=(pltpu.VMEM((1, 2 * rank, 2 * ran...  1.08 us
  transfers between devices with their start and end apart: 13, of which 8 were waited for; matrix products, arithmetic and copies ran while one was open for 0% of the time, Pallas kernels for 20%

profile of v2, /device:TPU:0, one launch (start us, length us, event | category | flops | bytes accessed | tf_op | source)
XLA Modules:
  0.0 35.0 jit_solution(1910620588891380916)
XLA Ops:
  0.0 0.0 copy-start
  0.0 2.8 %project.1 = (bf16[64,384]{1,0:T(8,128)(2,1)S(1)}, bf16[4096,384]{1,0:T(8,128)(2,1)S(1)}) custom-call(bf16[2,64,4096]{2,1,0:T(8,128)(2,1)} %bitcast.7, bf16[4096,384]{1,0:T(8,128)(2,1)} %rhs.1), custom_call_target="tpu_custom_call" | custom-call | flops 805306368 | bytes 4194304 | tf_op jit(solution)/shard_map/project/pallas_call | solution.py:77
  2.8 4.1 %collective-permute-start.1 = (bf16[64,384]{1,0:T(8,128)(2,1)S(1)}, bf16[64,384]{1,0:T(8,128)(2,1)S(1)}, u32[]{:S(2)}, u32[]{:S(2)}) collective-permute-start(bf16[64,384]{1,0:T(8,128)(2,1)S(1)} %get-tuple-element.18.after.skel), channel_id=1, source_target_pairs={{0,8},{1,9},{2,10},{3,11},{4,12},{5,13},{6,14},{7,15},{8,0},{9,1},... | collective-permute-start | bytes 147464 | tf_op jit(solution)/shard_map/ppermute | solution.py:20
  7.0 1.1 %mixers.1 = (bf16[1,128,128]{2,1,0:T(8,128)(2,1)S(1)}, bf16[3,128,128]{2,1,0:T(8,128)(2,1)S(1)}) custom-call(bf16[4,2,2,64,64]{4,3,2,1,0:T(8,128)(2,1)} %bitcast.9, s32[4,4]{1,0:T(4,128)} %bitcast.10, bf16[64,384]{1,0:T(8,128)(2,1)S(1)} %get-tuple-element.18.after.skel), custom_call_target="tpu_custom_call" | custom-call | flops 65536 | bytes 262144 | tf_op jit(solution)/shard_map/mixers/pallas_call | solution.py:113
  8.0 1.6 %collective-permute-start = (bf16[3,128,128]{2,1,0:T(8,128)(2,1)S(1)}, bf16[3,128,128]{2,1,0:T(8,128)(2,1)S(1)}, u32[]{:S(2)}, u32[]{:S(2)}) collective-permute-start(bf16[3,128,128]{2,1,0:T(8,128)(2,1)S(1)} %get-tuple-element.19.mix), channel_id=1, source_target_pairs={{0,2},{1,3},{2,0},{3,1},{4,6},{5,7},{6,4},{7,5},{8,10},{9,11},{10,... | collective-permute-start | bytes 294920 | tf_op jit(solution)/shard_map/ppermute | solution.py:20
  9.6 0.0 collective-permute-done.1.other
  9.6 0.3 level_step.1.skel
  9.9 2.3 %collective-permute-start.4 = (bf16[64,384]{1,0:T(8,128)(2,1)S(1)}, bf16[64,384]{1,0:T(8,128)(2,1)S(1)}, u32[]{:S(2)}, u32[]{:S(2)}) collective-permute-start(bf16[64,384]{1,0:T(8,128)(2,1)S(1)} %level_step.1.skel), channel_id=1, source_target_pairs={{0,6},{1,7},{2,4},{3,5},{4,2},{5,3},{6,0},{7,1},{8,14},{9,15},{10,... | collective-permute-start | bytes 147464 | tf_op jit(solution)/shard_map/ppermute | solution.py:20
  12.2 0.8 %collective-permute-start.3 = (bf16[64,384]{1,0:T(8,128)(2,1)S(1)}, bf16[64,384]{1,0:T(8,128)(2,1)S(1)}, u32[]{:S(2)}, u32[]{:S(2)}) collective-permute-start(bf16[64,384]{1,0:T(8,128)(2,1)S(1)} %level_step.1.skel), channel_id=1, source_target_pairs={{0,2},{1,3},{2,0},{3,1},{4,6},{5,7},{6,4},{7,5},{8,10},{9,11},{10,... | collective-permute-start | bytes 147464 | tf_op jit(solution)/shard_map/ppermute | solution.py:20
  13.0 0.4 %collective-permute-start.2 = (bf16[64,384]{1,0:T(8,128)(2,1)S(1)}, bf16[64,384]{1,0:T(8,128)(2,1)S(1)}, u32[]{:S(2)}, u32[]{:S(2)}) collective-permute-start(bf16[64,384]{1,0:T(8,128)(2,1)S(1)} %level_step.1.skel), channel_id=1, source_target_pairs={{0,4},{1,5},{2,6},{3,7},{4,0},{5,1},{6,2},{7,3},{8,12},{9,13},{10,... | collective-permute-start | bytes 147464 | tf_op jit(solution)/shard_map/ppermute | solution.py:20
  13.4 2.0 %collective-permute-done.4.skel_zy = bf16[64,384]{1,0:T(8,128)(2,1)S(1)} collective-permute-done((bf16[64,384]{1,0:T(8,128)(2,1)S(1)}, bf16[64,384]{1,0:T(8,128)(2,1)S(1)}, u32[]{:S(2)}, u32[]{:S(2)}) %collective-permute-start.4) | collective-permute-done | bytes 49184 | tf_op jit(solution)/shard_map/ppermute | solution.py:20
  15.5 0.8 %collective-permute-done.3.skel_y = bf16[64,384]{1,0:T(8,128)(2,1)S(1)} collective-permute-done((bf16[64,384]{1,0:T(8,128)(2,1)S(1)}, bf16[64,384]{1,0:T(8,128)(2,1)S(1)}, u32[]{:S(2)}, u32[]{:S(2)}) %collective-permute-start.3) | collective-permute-done | bytes 49184 | tf_op jit(solution)/shard_map/ppermute | solution.py:20
  16.3 0.8 %collective-permute-done.2.skel_z = bf16[64,384]{1,0:T(8,128)(2,1)S(1)} collective-permute-done((bf16[64,384]{1,0:T(8,128)(2,1)S(1)}, bf16[64,384]{1,0:T(8,128)(2,1)S(1)}, u32[]{:S(2)}, u32[]{:S(2)}) %collective-permute-start.2) | collective-permute-done | bytes 49184 | tf_op jit(solution)/shard_map/ppermute | solution.py:20
  17.1 0.0 collective-permute-done.mix_y
  17.1 0.6 %quad_step.1.pair = bf16[128,384]{1,0:T(8,128)(2,1)S(1)} custom-call(bf16[3,128,128]{2,1,0:T(8,128)(2,1)S(1)} %get-tuple-element.19.mix, bf16[3,128,128]{2,1,0:T(8,128)(2,1)S(1)} %collective-permute-done.mix_y, bf16[64,384]{1,0:T(8,128)(2,1)S(1)} %level_step.1.skel, bf16[64,384]{1,0:T(8,128)(2,1)S(1)} %collective-permute-done.2.skel_z, ...), custom_call_target="tpu_custom_call" | custom-call | flops 50331648 | bytes 294912 | tf_op jit(solution)/shard_map/quad_step/pallas_call | solution.py:228
  17.7 0.1 collective-permute-start.5
  17.8 1.3 %collective-permute-done.5.far = bf16[128,384]{1,0:T(8,128)(2,1)S(1)} collective-permute-done((bf16[128,384]{1,0:T(8,128)(2,1)S(1)}, bf16[128,384]{1,0:T(8,128)(2,1)S(1)}, u32[]{:S(2)}, u32[]{:S(2)}) %collective-permute-start.5) | collective-permute-done | bytes 98336 | tf_op jit(solution)/shard_map/ppermute | solution.py:20
  19.0 0.3 twin_step.1.after.refs_0_
  19.3 0.5 %collective-permute-start.11 = (bf16[128,384]{1,0:T(8,128)(2,1)S(1)}, bf16[128,384]{1,0:T(8,128)(2,1)S(1)}, u32[]{:S(2)}, u32[]{:S(2)}) collective-permute-start(bf16[128,384]{1,0:T(8,128)(2,1)S(1)} %twin_step.1.after.refs_0_), channel_id=1, source_target_pairs={{0,4},{1,5},{2,6},{3,7},{4,0},{5,1},{6,2},{7,3},{8,12},{9,13},{10,... | collective-permute-start | bytes 294920 | tf_op jit(solution)/shard_map/ppermute | solution.py:20
  19.9 2.4 %collective-permute-start.9 = (bf16[128,384]{1,0:T(8,128)(2,1)S(1)}, bf16[128,384]{1,0:T(8,128)(2,1)S(1)}, u32[]{:S(2)}, u32[]{:S(2)}) collective-permute-start(bf16[128,384]{1,0:T(8,128)(2,1)S(1)} %twin_step.1.after.refs_0_), channel_id=1, source_target_pairs={{0,8},{1,9},{2,10},{3,11},{4,12},{5,13},{6,14},{7,15},{8,0},{9,1},... | collective-permute-start | bytes 294920 | tf_op jit(solution)/shard_map/ppermute | solution.py:20
  22.3 1.5 %collective-permute-start.7 = (bf16[128,384]{1,0:T(8,128)(2,1)S(1)}, bf16[128,384]{1,0:T(8,128)(2,1)S(1)}, u32[]{:S(2)}, u32[]{:S(2)}) collective-permute-start(bf16[128,384]{1,0:T(8,128)(2,1)S(1)} %twin_step.1.after.refs_0_), channel_id=1, source_target_pairs={{0,12},{1,13},{2,14},{3,15},{4,8},{5,9},{6,10},{7,11},{8,4},{9,5},... | collective-permute-start | bytes 294920 | tf_op jit(solution)/shard_map/ppermute | solution.py:20
  23.8 0.0 collective-permute-start.6
  23.8 0.0 copy-done
  23.8 5.7 %behind.1 = (f32[4096,384]{1,0:T(8,128)S(1)}, bf16[4096,128]{1,0:T(8,128)(2,1)S(1)}, bf16[4,128,256]{2,1,0:T(8,128)(2,1)S(1)}) custom-call(bf16[2,16,256,256]{3,2,1,0:T(8,128)(2,1)} %near.1, bf16[4096,384]{1,0:T(8,128)(2,1)S(1)} %get-tuple-element.21.rhs_keep, bf16[2,64,4096]{2,1,0:T(8,128)(2,1)} %bitcast.6, bf16[16,2,64,64]{3,2,1,0:T(8,128)(2,1)} %bitcast.8, ...), custom_call_target="tpu_custom_call" | custom-call | flops 1610612736 | bytes 5767168 | tf_op jit(solution)/shard_map/behind/pallas_call | solution.py:176
  29.5 1.2 %collective-permute-done.7.refs_2_ = bf16[128,384]{1,0:T(8,128)(2,1)S(1)} collective-permute-done((bf16[128,384]{1,0:T(8,128)(2,1)S(1)}, bf16[128,384]{1,0:T(8,128)(2,1)S(1)}, u32[]{:S(2)}, u32[]{:S(2)}) %collective-permute-start.7) | collective-permute-done | bytes 98336 | tf_op jit(solution)/shard_map/ppermute | solution.py:20
  30.7 0.0 collective-permute-done.9.refs_4_
  30.7 0.0 collective-permute-done.11.refs_6_
  30.7 0.0 collective-permute-start.12
  30.8 0.5 %collective-permute-start.10 = (bf16[128,384]{1,0:T(8,128)(2,1)S(1)}, bf16[128,384]{1,0:T(8,128)(2,1)S(1)}, u32[]{:S(2)}, u32[]{:S(2)}) collective-permute-start(bf16[128,384]{1,0:T(8,128)(2,1)S(1)} %collective-permute-done.9.refs_4_), channel_id=1, source_target_pairs={{0,1},{1,0},{2,3},{3,2},{4,5},{5,4},{6,7},{7,6},{8,9},{9,8},{10,11... | collective-permute-start | bytes 294920 | tf_op jit(solution)/shard_map/ppermute | solution.py:20
  31.3 0.1 collective-permute-start.8
  31.3 0.0 collective-permute-done.6.refs_1_
  31.3 0.7 %collective-permute-done.12.refs_7_ = bf16[128,384]{1,0:T(8,128)(2,1)S(1)} collective-permute-done((bf16[128,384]{1,0:T(8,128)(2,1)S(1)}, bf16[128,384]{1,0:T(8,128)(2,1)S(1)}, u32[]{:S(2)}, u32[]{:S(2)}) %collective-permute-start.12) | collective-permute-done | bytes 98336 | tf_op jit(solution)/shard_map/ppermute | solution.py:20
  32.0 0.2 collective-permute-done.10.refs_5_
  32.2 0.4 %collective-permute-done.8.refs_3_ = bf16[128,384]{1,0:T(8,128)(2,1)S(1)} collective-permute-done((bf16[128,384]{1,0:T(8,128)(2,1)S(1)}, bf16[128,384]{1,0:T(8,128)(2,1)S(1)}, u32[]{:S(2)}, u32[]{:S(2)}) %collective-permute-start.8) | collective-permute-done | bytes 98336 | tf_op jit(solution)/shard_map/ppermute | solution.py:20
  32.6 2.4 %finish.1 = bf16[4096,384]{1,0:T(8,128)(2,1)} custom-call(bf16[128,384]{1,0:T(8,128)(2,1)S(1)} %twin_step.1.after.refs_0_, bf16[128,384]{1,0:T(8,128)(2,1)S(1)} %collective-permute-done.6.refs_1_, bf16[128,384]{1,0:T(8,128)(2,1)S(1)} %collective-permute-done.7.refs_2_, bf16[128,384]{1,0:T(8,128)(2,1)S(1)} %collective-permute-done.8.refs_3_, ...), custom_call_target="tpu_custom_call" | custom-call | flops 402653184 | bytes 9437184 | tf_op jit(solution)/shard_map/finish/pallas_call | solution.py:282
Async XLA Ops:
  0.0 23.8 %copy-start = (s32[1,16]{1,0:T(1,128)S(1)}, s32[1,16]{1,0:T(1,128)}, u32[]{:S(2)}) copy-start(s32[1,16]{1,0:T(1,128)} %order.1) | copy-start | bytes 196
  2.8 6.8 %collective-permute-start.1 = (bf16[64,384]{1,0:T(8,128)(2,1)S(1)}, bf16[64,384]{1,0:T(8,128)(2,1)S(1)}, u32[]{:S(2)}, u32[]{:S(2)}) collective-permute-start(bf16[64,384]{1,0:T(8,128)(2,1)S(1)} %get-tuple-element.18.after.skel), channel_id=1, source_target_pairs={{0,8},{1,9},{2,10},{3,11},{4,12},{5,13},{6,14},{7,15},{8,0},{9,1},... | collective-permute-start | bytes 147464 | tf_op jit(solution)/shard_map/ppermute | solution.py:20
  8.0 9.0 %collective-permute-start = (bf16[3,128,128]{2,1,0:T(8,128)(2,1)S(1)}, bf16[3,128,128]{2,1,0:T(8,128)(2,1)S(1)}, u32[]{:S(2)}, u32[]{:S(2)}) collective-permute-start(bf16[3,128,128]{2,1,0:T(8,128)(2,1)S(1)} %get-tuple-element.19.mix), channel_id=1, source_target_pairs={{0,2},{1,3},{2,0},{3,1},{4,6},{5,7},{6,4},{7,5},{8,10},{9,11},{10,... | collective-permute-start | bytes 294920 | tf_op jit(solution)/shard_map/ppermute | solution.py:20
  9.9 5.6 %collective-permute-start.4 = (bf16[64,384]{1,0:T(8,128)(2,1)S(1)}, bf16[64,384]{1,0:T(8,128)(2,1)S(1)}, u32[]{:S(2)}, u32[]{:S(2)}) collective-permute-start(bf16[64,384]{1,0:T(8,128)(2,1)S(1)} %level_step.1.skel), channel_id=1, source_target_pairs={{0,6},{1,7},{2,4},{3,5},{4,2},{5,3},{6,0},{7,1},{8,14},{9,15},{10,... | collective-permute-start | bytes 147464 | tf_op jit(solution)/shard_map/ppermute | solution.py:20
  12.2 4.1 %collective-permute-start.3 = (bf16[64,384]{1,0:T(8,128)(2,1)S(1)}, bf16[64,384]{1,0:T(8,128)(2,1)S(1)}, u32[]{:S(2)}, u32[]{:S(2)}) collective-permute-start(bf16[64,384]{1,0:T(8,128)(2,1)S(1)} %level_step.1.skel), channel_id=1, source_target_pairs={{0,2},{1,3},{2,0},{3,1},{4,6},{5,7},{6,4},{7,5},{8,10},{9,11},{10,... | collective-permute-start | bytes 147464 | tf_op jit(solution)/shard_map/ppermute | solution.py:20
  13.0 4.1 %collective-permute-start.2 = (bf16[64,384]{1,0:T(8,128)(2,1)S(1)}, bf16[64,384]{1,0:T(8,128)(2,1)S(1)}, u32[]{:S(2)}, u32[]{:S(2)}) collective-permute-start(bf16[64,384]{1,0:T(8,128)(2,1)S(1)} %level_step.1.skel), channel_id=1, source_target_pairs={{0,4},{1,5},{2,6},{3,7},{4,0},{5,1},{6,2},{7,3},{8,12},{9,13},{10,... | collective-permute-start | bytes 147464 | tf_op jit(solution)/shard_map/ppermute | solution.py:20
  17.7 1.4 %collective-permute-start.5 = (bf16[128,384]{1,0:T(8,128)(2,1)S(1)}, bf16[128,384]{1,0:T(8,128)(2,1)S(1)}, u32[]{:S(2)}, u32[]{:S(2)}) collective-permute-start(bf16[128,384]{1,0:T(8,128)(2,1)S(1)} %quad_step.1.pair), channel_id=1, source_target_pairs={{0,1},{1,0},{2,3},{3,2},{4,5},{5,4},{6,7},{7,6},{8,9},{9,8},{10,11... | collective-permute-start | bytes 294920 | tf_op jit(solution)/shard_map/ppermute | solution.py:20
  19.3 11.4 %collective-permute-start.11 = (bf16[128,384]{1,0:T(8,128)(2,1)S(1)}, bf16[128,384]{1,0:T(8,128)(2,1)S(1)}, u32[]{:S(2)}, u32[]{:S(2)}) collective-permute-start(bf16[128,384]{1,0:T(8,128)(2,1)S(1)} %twin_step.1.after.refs_0_), channel_id=1, source_target_pairs={{0,4},{1,5},{2,6},{3,7},{4,0},{5,1},{6,2},{7,3},{8,12},{9,13},{10,... | collective-permute-start | bytes 294920 | tf_op jit(solution)/shard_map/ppermute | solution.py:20
  19.9 10.9 %collective-permute-start.9 = (bf16[128,384]{1,0:T(8,128)(2,1)S(1)}, bf16[128,384]{1,0:T(8,128)(2,1)S(1)}, u32[]{:S(2)}, u32[]{:S(2)}) collective-permute-start(bf16[128,384]{1,0:T(8,128)(2,1)S(1)} %twin_step.1.after.refs_0_), channel_id=1, source_target_pairs={{0,8},{1,9},{2,10},{3,11},{4,12},{5,13},{6,14},{7,15},{8,0},{9,1},... | collective-permute-start | bytes 294920 | tf_op jit(solution)/shard_map/ppermute | solution.py:20
  22.3 8.5 %collective-permute-start.7 = (bf16[128,384]{1,0:T(8,128)(2,1)S(1)}, bf16[128,384]{1,0:T(8,128)(2,1)S(1)}, u32[]{:S(2)}, u32[]{:S(2)}) collective-permute-start(bf16[128,384]{1,0:T(8,128)(2,1)S(1)} %twin_step.1.after.refs_0_), channel_id=1, source_target_pairs={{0,12},{1,13},{2,14},{3,15},{4,8},{5,9},{6,10},{7,11},{8,4},{9,5},... | collective-permute-start | bytes 294920 | tf_op jit(solution)/shard_map/ppermute | solution.py:20
  23.8 7.5 %collective-permute-start.6 = (bf16[128,384]{1,0:T(8,128)(2,1)S(1)}, bf16[128,384]{1,0:T(8,128)(2,1)S(1)}, u32[]{:S(2)}, u32[]{:S(2)}) collective-permute-start(bf16[128,384]{1,0:T(8,128)(2,1)S(1)} %twin_step.1.after.refs_0_), channel_id=1, source_target_pairs={{0,1},{1,0},{2,3},{3,2},{4,5},{5,4},{6,7},{7,6},{8,9},{9,8},{10,11... | collective-permute-start | bytes 294920 | tf_op jit(solution)/shard_map/ppermute | solution.py:20
  30.7 1.3 %collective-permute-start.12 = (bf16[128,384]{1,0:T(8,128)(2,1)S(1)}, bf16[128,384]{1,0:T(8,128)(2,1)S(1)}, u32[]{:S(2)}, u32[]{:S(2)}) collective-permute-start(bf16[128,384]{1,0:T(8,128)(2,1)S(1)} %collective-permute-done.11.refs_6_), channel_id=1, source_target_pairs={{0,1},{1,0},{2,3},{3,2},{4,5},{5,4},{6,7},{7,6},{8,9},{9,8},{10,11... | collective-permute-start | bytes 294920 | tf_op jit(solution)/shard_map/ppermute | solution.py:20
  30.8 1.4 %collective-permute-start.10 = (bf16[128,384]{1,0:T(8,128)(2,1)S(1)}, bf16[128,384]{1,0:T(8,128)(2,1)S(1)}, u32[]{:S(2)}, u32[]{:S(2)}) collective-permute-start(bf16[128,384]{1,0:T(8,128)(2,1)S(1)} %collective-permute-done.9.refs_4_), channel_id=1, source_target_pairs={{0,1},{1,0},{2,3},{3,2},{4,5},{5,4},{6,7},{7,6},{8,9},{9,8},{10,11... | collective-permute-start | bytes 294920 | tf_op jit(solution)/shard_map/ppermute | solution.py:20
  31.3 1.3 %collective-permute-start.8 = (bf16[128,384]{1,0:T(8,128)(2,1)S(1)}, bf16[128,384]{1,0:T(8,128)(2,1)S(1)}, u32[]{:S(2)}, u32[]{:S(2)}) collective-permute-start(bf16[128,384]{1,0:T(8,128)(2,1)S(1)} %collective-permute-done.7.refs_2_), channel_id=1, source_target_pairs={{0,1},{1,0},{2,3},{3,2},{4,5},{5,4},{6,7},{7,6},{8,9},{9,8},{10,11... | collective-permute-start | bytes 294920 | tf_op jit(solution)/shard_map/ppermute | solution.py:20

commit v3 on v2

v3 whole, which is shorter than its diff:
```python
import functools

import jax
import jax.numpy as jnp
from jax import lax
from jax.experimental import pallas as pl
from jax.experimental.pallas import tpu as pltpu
from jax.sharding import PartitionSpec as P

BF = jnp.bfloat16
F32 = jnp.float32
VMEM = pl.BlockSpec(memory_space=pltpu.VMEM)
SMEM = pl.BlockSpec(memory_space=pltpu.SMEM)
ANY = pl.BlockSpec(memory_space=pl.ANY)
HBM = pl.BlockSpec(memory_space=pltpu.HBM)


def partner(array, apart):
    count = lax.axis_size("leaf")
    return lax.ppermute(array, "leaf", [(i, i ^ apart) for i in range(count)])


def in_hbm(array):
    return pltpu.with_memory_space_constraint(array, pltpu.HBM)


def turned(block):
    half = block.shape[1] // 2
    return jnp.concatenate([-block[:, half:], block[:, :half]], axis=1)


def combined(stacked):
    rank = stacked.shape[0] // 2
    return stacked[:rank] + turned(stacked[rank:])


def dot(a, b):
    return jnp.dot(a, b, preferred_element_type=F32)


def params(mib):
    return pltpu.CompilerParams(vmem_limit_bytes=mib * 2**20)


def cost(flops, moved):
    return pl.CostEstimate(flops=flops, bytes_accessed=moved, transcendentals=0)


def open_kernel(cuts, orders, left, rhs, factors, pattern, coupling, order, here, *refs):
    skel, rhs_keep, first, rest = refs[:4]
    tables = refs[4:4 + len(orders)]
    left_buf, fac_buf, pat_buf, couple_buf, order_buf, slot, sems = refs[4 + len(orders):]
    levels, blocks = pattern.shape
    rank = left.shape[1]
    high = rank // blocks
    ahead = (
        pltpu.make_async_copy(factors, fac_buf, sems.at[0]),
        pltpu.make_async_copy(pattern, pat_buf, sems.at[1]),
        pltpu.make_async_copy(order, order_buf, sems.at[2]),
        pltpu.make_async_copy(coupling, couple_buf, sems.at[3]),
    )
    copies = []
    start = 0
    for c, depth in enumerate(cuts):
        span = pl.ds(start, depth)
        copies.append((
            span,
            pltpu.make_async_copy(left.at[:, :, span], left_buf.at[:, :, span], sems.at[4 + 2 * c]),
            pltpu.make_async_copy(rhs.at[span], rhs_keep.at[span], sems.at[5 + 2 * c]),
        ))
        start += depth
    for copy in ahead:
        copy.start()
    for _, one, two in copies:
        one.start()
        two.start()
    ahead[0].wait()
    ahead[1].wait()
    for level in range(levels):
        out, at = (first, 0) if level == 0 else (rest, level - 1)
        for part in range(2):
            own = fac_buf[level, 0, part]
            cross = fac_buf[level, 1, part].astype(F32)
            pieces = [cross[r * high:(r + 1) * high, :] * pat_buf[level, r].astype(F32) for r in range(blocks)]
            masked = jnp.concatenate(pieces, axis=0).astype(BF)
            out[at, pl.ds(part * rank, rank), :] = jnp.concatenate([own, masked], axis=1)
    ahead[2].wait()
    for j in range(coupling.shape[0]):
        slot[order_buf[0, j] ^ here[0]] = j
    ahead[3].wait()
    for members, table in zip(orders, tables):
        for part in range(2):
            for i in range(0, len(members), 2):
                pair = [couple_buf[slot[m], part] for m in members[i:i + 2]]
                table[pl.ds(part * rank, rank), pl.ds(i * rank, 2 * rank)] = jnp.concatenate(pair, axis=1)
    total = None
    for span, one, two in copies:
        one.wait()
        two.wait()
        term = dot(left_buf[:, :, span].reshape(2 * rank, span.size), rhs_keep[span, :])
        total = term if total is None else total + term
    skel[...] = combined(total).astype(BF)


def open_step(left_t, rhs, factors, pattern, coupling, order, here, orders):
    rank = left_t.shape[1]
    rows = rhs.shape[0]
    cuts = (rows // 2, rows // 4, rows // 4)
    levels = factors.shape[0]
    outs = (
        pltpu.VMEM((rank, rhs.shape[1]), BF),
        pltpu.VMEM(rhs.shape, BF),
        pltpu.VMEM((1, 2 * rank, 2 * rank), BF),
        pltpu.VMEM((levels - 1, 2 * rank, 2 * rank), BF),
    ) + tuple(pltpu.VMEM((2 * rank, len(members) * rank), BF) for members in orders)
    return pl.pallas_call(
        functools.partial(open_kernel, cuts, orders),
        out_shape=outs,
        in_specs=[HBM] * 6 + [SMEM],
        out_specs=tuple(VMEM for _ in outs),
        scratch_shapes=[
            pltpu.VMEM(left_t.shape, BF),
            pltpu.VMEM(factors.shape, BF),
            pltpu.SMEM(pattern.shape, jnp.int32),
            pltpu.VMEM(coupling.shape, BF),
            pltpu.SMEM(order.shape, jnp.int32),
            pltpu.SMEM((coupling.shape[0],), jnp.int32),
            pltpu.SemaphoreType.DMA((4 + 2 * len(cuts),)),
        ],
        compiler_params=params(6),
        cost_estimate=cost(4 * left_t.size * rhs.shape[1], 2 * (left_t.size + rhs.size)),
        name="open_step",
    )(left_t, rhs, factors, pattern, coupling, order, here)


def near_kernel(groups, near, rhs, after, out, buf, sems):
    boxes, width = near.shape[1], near.shape[2]
    each = boxes // groups
    copies = []
    for g in range(groups):
        span = pl.ds(g * each, each)
        copies.append(pltpu.make_async_copy(near.at[:, span], buf.at[:, span], sems.at[g]))
        copies[-1].start()
    for g in range(groups):
        copies[g].wait()
        for b in range(g * each, (g + 1) * each):
            rows_b = pl.ds(b * width, width)
            block = rhs[rows_b, :]
            out[rows_b, :] = dot(buf[0, b], block) + dot(buf[1, b], turned(block))


def near_term(near, rhs, after):
    groups = 4
    rows, cols = rhs.shape
    return pl.pallas_call(
        functools.partial(near_kernel, groups),
        out_shape=pltpu.VMEM((rows, cols), F32),
        in_specs=[HBM, VMEM, ANY],
        out_specs=VMEM,
        scratch_shapes=[pltpu.VMEM(near.shape, BF), pltpu.SemaphoreType.DMA((groups,))],
        compiler_params=params(8),
        cost_estimate=cost(4 * rows * near.shape[2] * cols, 2 * near.size),
        name="near_term",
    )(near, rhs, after)


def mixed(matrix, one, two):
    return combined(dot(matrix, jnp.concatenate([one, two], axis=0))).astype(BF)


def level_kernel(level, mixers, skel, other, out):
    out[...] = mixed(mixers[level], skel[...], other[...])


def level_step(level, mixers, skel, other):
    return pl.pallas_call(
        functools.partial(level_kernel, level),
        out_shape=pltpu.VMEM(skel.shape, BF),
        in_specs=[VMEM, VMEM, VMEM],
        out_specs=VMEM,
        compiler_params=params(1),
        cost_estimate=cost(8 * skel.shape[0] * skel.size, 6 * skel.size),
        name="level_step",
    )(mixers, skel, other)


def quad_kernel(mix, mix_y, skel, skel_y, skel_zy, skel_z, out):
    rank = skel.shape[0]
    here = mixed(mix[0], skel[...], skel_z[...])
    there = mixed(mix_y[0], skel_y[...], skel_zy[...])
    out[:rank, :] = mixed(mix[1], here, there)
    out[rank:, :] = mixed(mix_y[1], there, here)


def quad_step(mix, mix_y, skel, skel_y, skel_zy, skel_z):
    rank, cols = skel.shape
    return pl.pallas_call(
        quad_kernel,
        out_shape=pltpu.VMEM((2 * rank, cols), BF),
        in_specs=[VMEM] * 6,
        out_specs=VMEM,
        compiler_params=params(1),
        cost_estimate=cost(32 * rank * skel.size, 12 * skel.size),
        name="quad_step",
    )(mix, mix_y, skel, skel_y, skel_zy, skel_z)


def twin_kernel(mix, mix_y, pair, far, out):
    rank = pair.shape[0] // 2
    out[:rank, :] = mixed(mix[2], pair[:rank, :], far[:rank, :])
    out[rank:, :] = mixed(mix_y[2], pair[rank:, :], far[rank:, :])


def twin_step(mix, mix_y, pair, far):
    return pl.pallas_call(
        twin_kernel,
        out_shape=pltpu.VMEM(pair.shape, BF),
        in_specs=[VMEM] * 4,
        out_specs=VMEM,
        compiler_params=params(1),
        cost_estimate=cost(8 * pair.shape[0] * pair.size, 8 * pair.size),
        name="twin_step",
    )(mix, mix_y, pair, far)


def couple_kernel(n_blocks, *refs):
    blocks, rest = refs[:n_blocks], refs[n_blocks:]
    half = len(rest) // 2
    stack = jnp.concatenate([ref[...] for ref in blocks], axis=0)
    for table, out in zip(rest[:half], rest[half:]):
        out[...] = combined(dot(table[...], stack))


def couple_step(blocks, tables):
    rank, cols = tables[0].shape[0] // 2, blocks[0].shape[1]
    outs = tuple(pltpu.VMEM((rank, cols), F32) for _ in tables)
    return pl.pallas_call(
        functools.partial(couple_kernel, len(blocks)),
        out_shape=outs,
        in_specs=[VMEM] * (len(blocks) + len(tables)),
        out_specs=tuple(VMEM for _ in outs),
        compiler_params=params(3),
        cost_estimate=cost(2 * len(tables) * tables[0].size * cols, 4 * rank * cols),
        name="couple_step",
    )(*blocks, *tables)


def finish_kernel(n_sums, chunks, *refs):
    sums = refs[:n_sums]
    near, right, out, buf, sems = refs[n_sums:]
    rank, rows = right.shape[1:]
    total = sums[0][...]
    for ref in sums[1:]:
        total += ref[...]
    coarse = total.astype(BF)
    weights = jnp.concatenate([coarse, turned(coarse)], axis=0)
    depth = rows // chunks
    copies = []
    for c in range(chunks):
        span = pl.ds(c * depth, depth)
        basis = right[:, :, span].reshape(2 * rank, depth)
        far = lax.dot_general(basis, weights, (((0,), (0,)), ((), ())), preferred_element_type=F32)
        buf[span, :] = (far + near[span, :]).astype(BF)
        copies.append(pltpu.make_async_copy(buf.at[span], out.at[span], sems.at[c]))
        copies[-1].start()
    for copy in copies:
        copy.wait()


def finish(sums, near, right_t):
    chunks = 8
    rows, cols = near.shape
    return pl.pallas_call(
        functools.partial(finish_kernel, len(sums), chunks),
        out_shape=jax.ShapeDtypeStruct((rows, cols), BF),
        in_specs=[VMEM] * (len(sums) + 2),
        out_specs=ANY,
        scratch_shapes=[pltpu.VMEM((rows, cols), BF), pltpu.SemaphoreType.DMA((chunks,))],
        compiler_params=params(6),
        cost_estimate=cost(2 * right_t.size * cols, 6 * rows * cols),
        name="finish",
    )(*sums, near, right_t)


def per_device(rhs, left_basis, right_basis, near_field, factors, coupling, pattern, leaf_order):
    leaves = lax.axis_size("leaf")
    bits = leaves.bit_length() - 1
    levels = factors.shape[1]
    group = leaf_order.shape[1]
    left_t = in_hbm(jnp.swapaxes(left_basis, 1, 2))
    right_t = jnp.swapaxes(right_basis, 1, 2)
    near_field = in_hbm(near_field)
    here = (lax.axis_index("leaf") & (group - 1)).astype(jnp.int32)[None]
    begin = functools.partial(open_step, left_t, in_hbm(rhs), in_hbm(factors[0]), in_hbm(pattern[0]), in_hbm(coupling[0]),
                              in_hbm(leaf_order), here)

    if leaves == group == 16 and levels == 4:
        far_order = (8, 4, 12)
        names = []
        for base in (0,) + far_order:
            names += [base, base ^ 2]
        skel, kept, first, rest, table, table_core = begin((tuple(names), tuple(n ^ 1 for n in names)))
        table_core = partner(table_core, 1)
        rest_y = partner(rest, 2)
        skel = level_step(0, first, skel, partner(skel, 8))
        side = {apart: partner(skel, apart) for apart in (4, 2, 6)}
        pair = quad_step(rest, rest_y, skel, side[2], side[6], side[4])
        pair = twin_step(rest, rest_y, pair, partner(pair, 1))
        far = [partner(pair, apart) for apart in far_order]
        near = near_term(near_field, kept, pair)
        *far, near = lax.optimization_barrier((*far, near))
        total_core, total = couple_step([pair] + far, [table_core, table])
        sums = [total, partner(total_core, 1)]
    else:
        names = (0,)
        for bit in reversed(range(group.bit_length() - 1)):
            names = names + tuple(n ^ (1 << bit) for n in names)
        skel, kept, first, rest, table = begin((names,))
        for level in range(levels):
            matrix, at = (first, 0) if level == 0 else (rest, level - 1)
            skel = level_step(at, matrix, skel, partner(skel, 1 << (bits - 1 - level)))
        blocks = [skel]
        for bit in reversed(range(group.bit_length() - 1)):
            other = partner(jnp.stack(blocks), 1 << bit)
            blocks = blocks + [other[i] for i in range(len(blocks))]
        near = near_term(near_field, kept, skel)
        sums = couple_step(blocks, [table])
    return finish(sums, near, right_t)


def solution(mesh):
    both = ("parts", "leaf")
    in_specs = (
        P(both, None),
        P(None, both, None),
        P(None, both, None),
        P(None, both, None, None),
        P(both, None, None, None, None, None),
        P(both, None, None, None, None),
        P(both, None, None),
        P(both, None),
    )
    return jax.shard_map(
        per_device, mesh=mesh, in_specs=in_specs, out_specs=P(both, None), check_vma=False
    )
```

time: 35.1 us -> 34.6 us (0.986)
  Pallas kernels: 13.2 us -> 11.5 us
  waiting for transfers between devices: 7.36 us -> 8.55 us
    pallas_call x4, Pallas kernels: 12.1 us -> 10.3 us  [the longest x1 4.78 us: near_term(): pl.pallas_call(functools.partial(near_kernel, groups), out_shape=pltpu.VM...]
    ppermute x13 -> x11, waiting for transfers between devices: 7.36 us -> 8.55 us  [partner(): return lax.ppermute(array, 'leaf', [(i, i ^ apart) for i in range(count)])]
    ppermute x13 -> x11, starting transfers between devices: 14.3 us -> 14.4 us  [partner(): return lax.ppermute(array, 'leaf', [(i, i ^ apart) for i in range(count)])]
  transfers between devices with their start and end apart: 13 -> 11, of which waited for: 8 -> 7; matrix products, arithmetic and copies ran while one was open for 0% -> 0% of each run, Pallas kernels for 20% -> 15%
where the time goes in v3:
time: 34.6 us; the launch traced here: 34.5 us
  starting transfers between devices  14.4 us (42%)
  Pallas kernels  11.5 us (33%)
  waiting for transfers between devices  8.55 us (25%)
    ppermute x11, starting transfers between devices, partner(): return lax.ppermute(array, 'leaf', [(i, i ^ apart) for i in range(count)])  14.4 us
    ppermute x11, waiting for transfers between devices, partner(): return lax.ppermute(array, 'leaf', [(i, i ^ apart) for i in range(count)])  8.55 us
    pallas_call x1, Pallas kernels, near_term(): pl.pallas_call(functools.partial(near_kernel, groups), out_shape=pltpu.VM...  4.78 us
    pallas_call x1, Pallas kernels, open_step(): pl.pallas_call(functools.partial(open_kernel, cuts, orders), out_shape=ou...  3.1 us
    pallas_call x1, Pallas kernels, finish(): pl.pallas_call(functools.partial(finish_kernel, len(sums), chunks), out_s...  2.08 us
  transfers between devices with their start and end apart: 11, of which 7 were waited for; matrix products, arithmetic and copies ran while one was open for 0% of the time, Pallas kernels for 15%

profile of v3, /device:TPU:0, one launch (start us, length us, event | category | flops | bytes accessed | tf_op | source)
XLA Modules:
  0.0 34.5 jit_solution(1650084247343608416)
XLA Ops:
  0.0 3.1 %open_step.1 = (bf16[64,384]{1,0:T(8,128)(2,1)S(1)}, bf16[4096,384]{1,0:T(8,128)(2,1)S(1)}, bf16[1,128,128]{2,1,0:T(8,128)(2,1)S(1)}, bf16[3,128,128]{2,1,0:T(8,...) custom-call(bf16[2,64,4096]{2,1,0:T(8,128)(2,1)} %bitcast.7, bf16[4096,384]{1,0:T(8,128)(2,1)} %rhs.1, ...), custom_call_target="tpu_custom_call" | custom-call | flops 805306368 | bytes 4194304 | tf_op jit(solution)/shard_map/open_step/pallas_call | solution.py:116
  3.1 4.1 %collective-permute-start.1 = (bf16[64,384]{1,0:T(8,128)(2,1)S(1)}, bf16[64,384]{1,0:T(8,128)(2,1)S(1)}, u32[]{:S(2)}, u32[]{:S(2)}) collective-permute-start(bf16[64,384]{1,0:T(8,128)(2,1)S(1)} %get-tuple-element.19.skel), channel_id=1, source_target_pairs={{0,8},{1,9},{2,10},{3,11},{4,12},{5,13},{6,14},{7,15},{8,0},{9,1},... | collective-permute-start | bytes 147464 | tf_op jit(solution)/shard_map/ppermute | solution.py:20
  7.2 1.5 %collective-permute-start = (bf16[3,128,128]{2,1,0:T(8,128)(2,1)S(1)}, bf16[3,128,128]{2,1,0:T(8,128)(2,1)S(1)}, u32[]{:S(2)}, u32[]{:S(2)}) collective-permute-start(bf16[3,128,128]{2,1,0:T(8,128)(2,1)S(1)} %get-tuple-element.17.mix), channel_id=1, source_target_pairs={{0,2},{1,3},{2,0},{3,1},{4,6},{5,7},{6,4},{7,5},{8,10},{9,11},{10,... | collective-permute-start | bytes 294920 | tf_op jit(solution)/shard_map/ppermute | solution.py:20
  8.7 1.1 %collective-permute-done.1.other = bf16[64,384]{1,0:T(8,128)(2,1)S(1)} collective-permute-done((bf16[64,384]{1,0:T(8,128)(2,1)S(1)}, bf16[64,384]{1,0:T(8,128)(2,1)S(1)}, u32[]{:S(2)}, u32[]{:S(2)}) %collective-permute-start.1) | collective-permute-done | bytes 49184 | tf_op jit(solution)/shard_map/ppermute | solution.py:20
  9.8 0.3 level_step.1.skel
  10.1 1.8 %collective-permute-start.2 = (bf16[64,384]{1,0:T(8,128)(2,1)S(1)}, bf16[64,384]{1,0:T(8,128)(2,1)S(1)}, u32[]{:S(2)}, u32[]{:S(2)}) collective-permute-start(bf16[64,384]{1,0:T(8,128)(2,1)S(1)} %level_step.1.skel), channel_id=1, source_target_pairs={{0,2},{1,3},{2,0},{3,1},{4,6},{5,7},{6,4},{7,5},{8,10},{9,11},{10,... | collective-permute-start | bytes 147464 | tf_op jit(solution)/shard_map/ppermute | solution.py:20
  11.9 1.1 %collective-permute-start.3 = (bf16[64,384]{1,0:T(8,128)(2,1)S(1)}, bf16[64,384]{1,0:T(8,128)(2,1)S(1)}, u32[]{:S(2)}, u32[]{:S(2)}) collective-permute-start(bf16[64,384]{1,0:T(8,128)(2,1)S(1)} %level_step.1.skel), channel_id=1, source_target_pairs={{0,6},{1,7},{2,4},{3,5},{4,2},{5,3},{6,0},{7,1},{8,14},{9,15},{10,... | collective-permute-start | bytes 147464 | tf_op jit(solution)/shard_map/ppermute | solution.py:20
  13.0 0.7 %collective-permute-start.4 = (bf16[64,384]{1,0:T(8,128)(2,1)S(1)}, bf16[64,384]{1,0:T(8,128)(2,1)S(1)}, u32[]{:S(2)}, u32[]{:S(2)}) collective-permute-start(bf16[64,384]{1,0:T(8,128)(2,1)S(1)} %level_step.1.skel), channel_id=1, source_target_pairs={{0,4},{1,5},{2,6},{3,7},{4,0},{5,1},{6,2},{7,3},{8,12},{9,13},{10,... | collective-permute-start | bytes 147464 | tf_op jit(solution)/shard_map/ppermute | solution.py:20
  13.6 0.8 %collective-permute-done.2.skel_y = bf16[64,384]{1,0:T(8,128)(2,1)S(1)} collective-permute-done((bf16[64,384]{1,0:T(8,128)(2,1)S(1)}, bf16[64,384]{1,0:T(8,128)(2,1)S(1)}, u32[]{:S(2)}, u32[]{:S(2)}) %collective-permute-start.2) | collective-permute-done | bytes 49184 | tf_op jit(solution)/shard_map/ppermute | solution.py:20
  14.4 2.4 %collective-permute-done.3.skel_zy = bf16[64,384]{1,0:T(8,128)(2,1)S(1)} collective-permute-done((bf16[64,384]{1,0:T(8,128)(2,1)S(1)}, bf16[64,384]{1,0:T(8,128)(2,1)S(1)}, u32[]{:S(2)}, u32[]{:S(2)}) %collective-permute-start.3) | collective-permute-done | bytes 49184 | tf_op jit(solution)/shard_map/ppermute | solution.py:20
  16.9 0.2 collective-permute-done.4.skel_z
  17.1 0.0 collective-permute-done.mix_y
  17.1 0.6 %quad_step.1.pair = bf16[128,384]{1,0:T(8,128)(2,1)S(1)} custom-call(bf16[3,128,128]{2,1,0:T(8,128)(2,1)S(1)} %get-tuple-element.17.mix, bf16[3,128,128]{2,1,0:T(8,128)(2,1)S(1)} %collective-permute-done.mix_y, bf16[64,384]{1,0:T(8,128)(2,1)S(1)} %level_step.1.skel, bf16[64,384]{1,0:T(8,128)(2,1)S(1)} %collective-permute-done.2.skel_y, ...), custom_call_target="tpu_custom_call" | custom-call | flops 50331648 | bytes 294912 | tf_op jit(solution)/shard_map/quad_step/pallas_call | solution.py:197
  17.7 0.1 collective-permute-start.5
  17.7 0.5 %collective-permute-start.9 = (bf16[128,512]{1,0:T(8,128)(2,1)S(1)}, bf16[128,512]{1,0:T(8,128)(2,1)S(1)}, u32[]{:S(2)}, u32[]{:S(2)}) collective-permute-start(bf16[128,512]{1,0:T(8,128)(2,1)S(1)} %get-tuple-element.24), channel_id=1, source_target_pairs={{0,1},{1,0},{2,3},{3,2},{4,5},{5,4},{6,7},{7,6},{8,9},{9,8},{10,11... | collective-permute-start | bytes 393224 | tf_op jit(solution)/shard_map/ppermute | solution.py:20
  18.2 0.8 %collective-permute-done.5.far = bf16[128,384]{1,0:T(8,128)(2,1)S(1)} collective-permute-done((bf16[128,384]{1,0:T(8,128)(2,1)S(1)}, bf16[128,384]{1,0:T(8,128)(2,1)S(1)}, u32[]{:S(2)}, u32[]{:S(2)}) %collective-permute-start.5) | collective-permute-done | bytes 98336 | tf_op jit(solution)/shard_map/ppermute | solution.py:20
  19.0 0.3 twin_step.1.after.refs_0_
  19.3 3.1 %collective-permute-start.6 = (bf16[128,384]{1,0:T(8,128)(2,1)S(1)}, bf16[128,384]{1,0:T(8,128)(2,1)S(1)}, u32[]{:S(2)}, u32[]{:S(2)}) collective-permute-start(bf16[128,384]{1,0:T(8,128)(2,1)S(1)} %twin_step.1.after.refs_0_), channel_id=1, source_target_pairs={{0,8},{1,9},{2,10},{3,11},{4,12},{5,13},{6,14},{7,15},{8,0},{9,1},... | collective-permute-start | bytes 294920 | tf_op jit(solution)/shard_map/ppermute | solution.py:20
  22.4 1.0 %collective-permute-start.7 = (bf16[128,384]{1,0:T(8,128)(2,1)S(1)}, bf16[128,384]{1,0:T(8,128)(2,1)S(1)}, u32[]{:S(2)}, u32[]{:S(2)}) collective-permute-start(bf16[128,384]{1,0:T(8,128)(2,1)S(1)} %twin_step.1.after.refs_0_), channel_id=1, source_target_pairs={{0,4},{1,5},{2,6},{3,7},{4,0},{5,1},{6,2},{7,3},{8,12},{9,13},{10,... | collective-permute-start | bytes 294920 | tf_op jit(solution)/shard_map/ppermute | solution.py:20
  23.3 0.6 %collective-permute-start.8 = (bf16[128,384]{1,0:T(8,128)(2,1)S(1)}, bf16[128,384]{1,0:T(8,128)(2,1)S(1)}, u32[]{:S(2)}, u32[]{:S(2)}) collective-permute-start(bf16[128,384]{1,0:T(8,128)(2,1)S(1)} %twin_step.1.after.refs_0_), channel_id=1, source_target_pairs={{0,12},{1,13},{2,14},{3,15},{4,8},{5,9},{6,10},{7,11},{8,4},{9,5},... | collective-permute-start | bytes 294920 | tf_op jit(solution)/shard_map/ppermute | solution.py:20
  23.9 0.0 copy-start
  23.9 4.8 %near_term.1.refs_2_ = f32[4096,384]{1,0:T(8,128)S(1)} custom-call(bf16[2,16,256,256]{3,2,1,0:T(8,128)(2,1)} %near.1, bf16[4096,384]{1,0:T(8,128)(2,1)S(1)} %get-tuple-element.20.rhs, bf16[128,384]{1,0:T(8,128)(2,1)S(1)} %twin_step.1.after.refs_0_), custom_call_target="tpu_custom_call" | custom-call | flops 1610612736 | bytes 4194304 | tf_op jit(solution)/shard_map/near_term/pallas_call | solution.py:155
  28.7 0.0 collective-permute-done.6.refs_1_
  28.7 1.9 %collective-permute-done.7.refs_2_ = bf16[128,384]{1,0:T(8,128)(2,1)S(1)} collective-permute-done((bf16[128,384]{1,0:T(8,128)(2,1)S(1)}, bf16[128,384]{1,0:T(8,128)(2,1)S(1)}, u32[]{:S(2)}, u32[]{:S(2)}) %collective-permute-start.7) | collective-permute-done | bytes 98336 | tf_op jit(solution)/shard_map/ppermute | solution.py:20
  30.7 0.0 collective-permute-done.8.refs_3_
  30.7 0.0 collective-permute-done.9.refs_4_
  30.7 0.4 %couple_step.1 = (f32[64,384]{1,0:T(8,128)S(1)}, f32[64,384]{1,0:T(8,128)S(1)}) custom-call(bf16[128,384]{1,0:T(8,128)(2,1)S(1)} %twin_step.1.after.refs_0_, bf16[128,384]{1,0:T(8,128)(2,1)S(1)} %collective-permute-done.6.refs_1_, bf16[128,384]{1,0:T(8,128)(2,1)S(1)} %collective-permute-done.7.refs_2_, bf16[128,384]{1,0:T(8,128)(2,1)S(1)} %collective-permute-done.8.refs_3_, ...), custom_call_target="tpu_custom_call" | custom-call | flops 100663296 | bytes 98304 | tf_op jit(solution)/shard_map/couple_step/pallas_call | solution.py:237
  31.1 0.1 collective-permute-start.10
  31.1 1.3 %collective-permute-done.10.refs_1_ = f32[64,384]{1,0:T(8,128)S(1)} collective-permute-done((f32[64,384]{1,0:T(8,128)S(1)}, f32[64,384]{1,0:T(8,128)S(1)}, u32[]{:S(2)}, u32[]{:S(2)}) %collective-permute-start.10) | collective-permute-done | bytes 98336 | tf_op jit(solution)/shard_map/ppermute | solution.py:20
  32.4 0.0 copy-done
  32.4 2.1 %finish.1 = bf16[4096,384]{1,0:T(8,128)(2,1)} custom-call(f32[64,384]{1,0:T(8,128)S(1)} %get-tuple-element.26.refs_0_, f32[64,384]{1,0:T(8,128)S(1)} %collective-permute-done.10.refs_1_, f32[4096,384]{1,0:T(8,128)S(1)} %near_term.1.refs_2_, bf16[2,64,4096]{2,1,0:T(8,128)(2,1)S(1)} %bitcast.6), custom_call_target="tpu_custom_call" | custom-call | flops 402653184 | bytes 9437184 | tf_op jit(solution)/shard_map/finish/pallas_call | solution.py:273
Async XLA Ops:
  3.1 6.7 %collective-permute-start.1 = (bf16[64,384]{1,0:T(8,128)(2,1)S(1)}, bf16[64,384]{1,0:T(8,128)(2,1)S(1)}, u32[]{:S(2)}, u32[]{:S(2)}) collective-permute-start(bf16[64,384]{1,0:T(8,128)(2,1)S(1)} %get-tuple-element.19.skel), channel_id=1, source_target_pairs={{0,8},{1,9},{2,10},{3,11},{4,12},{5,13},{6,14},{7,15},{8,0},{9,1},... | collective-permute-start | bytes 147464 | tf_op jit(solution)/shard_map/ppermute | solution.py:20
  7.2 9.9 %collective-permute-start = (bf16[3,128,128]{2,1,0:T(8,128)(2,1)S(1)}, bf16[3,128,128]{2,1,0:T(8,128)(2,1)S(1)}, u32[]{:S(2)}, u32[]{:S(2)}) collective-permute-start(bf16[3,128,128]{2,1,0:T(8,128)(2,1)S(1)} %get-tuple-element.17.mix), channel_id=1, source_target_pairs={{0,2},{1,3},{2,0},{3,1},{4,6},{5,7},{6,4},{7,5},{8,10},{9,11},{10,... | collective-permute-start | bytes 294920 | tf_op jit(solution)/shard_map/ppermute | solution.py:20
  10.1 4.3 %collective-permute-start.2 = (bf16[64,384]{1,0:T(8,128)(2,1)S(1)}, bf16[64,384]{1,0:T(8,128)(2,1)S(1)}, u32[]{:S(2)}, u32[]{:S(2)}) collective-permute-start(bf16[64,384]{1,0:T(8,128)(2,1)S(1)} %level_step.1.skel), channel_id=1, source_target_pairs={{0,2},{1,3},{2,0},{3,1},{4,6},{5,7},{6,4},{7,5},{8,10},{9,11},{10,... | collective-permute-start | bytes 147464 | tf_op jit(solution)/shard_map/ppermute | solution.py:20
  11.9 5.0 %collective-permute-start.3 = (bf16[64,384]{1,0:T(8,128)(2,1)S(1)}, bf16[64,384]{1,0:T(8,128)(2,1)S(1)}, u32[]{:S(2)}, u32[]{:S(2)}) collective-permute-start(bf16[64,384]{1,0:T(8,128)(2,1)S(1)} %level_step.1.skel), channel_id=1, source_target_pairs={{0,6},{1,7},{2,4},{3,5},{4,2},{5,3},{6,0},{7,1},{8,14},{9,15},{10,... | collective-permute-start | bytes 147464 | tf_op jit(solution)/shard_map/ppermute | solution.py:20
  13.0 4.1 %collective-permute-start.4 = (bf16[64,384]{1,0:T(8,128)(2,1)S(1)}, bf16[64,384]{1,0:T(8,128)(2,1)S(1)}, u32[]{:S(2)}, u32[]{:S(2)}) collective-permute-start(bf16[64,384]{1,0:T(8,128)(2,1)S(1)} %level_step.1.skel), channel_id=1, source_target_pairs={{0,4},{1,5},{2,6},{3,7},{4,0},{5,1},{6,2},{7,3},{8,12},{9,13},{10,... | collective-permute-start | bytes 147464 | tf_op jit(solution)/shard_map/ppermute | solution.py:20
  17.7 1.4 %collective-permute-start.5 = (bf16[128,384]{1,0:T(8,128)(2,1)S(1)}, bf16[128,384]{1,0:T(8,128)(2,1)S(1)}, u32[]{:S(2)}, u32[]{:S(2)}) collective-permute-start(bf16[128,384]{1,0:T(8,128)(2,1)S(1)} %quad_step.1.pair), channel_id=1, source_target_pairs={{0,1},{1,0},{2,3},{3,2},{4,5},{5,4},{6,7},{7,6},{8,9},{9,8},{10,11... | collective-permute-start | bytes 294920 | tf_op jit(solution)/shard_map/ppermute | solution.py:20
  17.7 12.9 %collective-permute-start.9 = (bf16[128,512]{1,0:T(8,128)(2,1)S(1)}, bf16[128,512]{1,0:T(8,128)(2,1)S(1)}, u32[]{:S(2)}, u32[]{:S(2)}) collective-permute-start(bf16[128,512]{1,0:T(8,128)(2,1)S(1)} %get-tuple-element.24), channel_id=1, source_target_pairs={{0,1},{1,0},{2,3},{3,2},{4,5},{5,4},{6,7},{7,6},{8,9},{9,8},{10,11... | collective-permute-start | bytes 393224 | tf_op jit(solution)/shard_map/ppermute | solution.py:20
  19.3 9.4 %collective-permute-start.6 = (bf16[128,384]{1,0:T(8,128)(2,1)S(1)}, bf16[128,384]{1,0:T(8,128)(2,1)S(1)}, u32[]{:S(2)}, u32[]{:S(2)}) collective-permute-start(bf16[128,384]{1,0:T(8,128)(2,1)S(1)} %twin_step.1.after.refs_0_), channel_id=1, source_target_pairs={{0,8},{1,9},{2,10},{3,11},{4,12},{5,13},{6,14},{7,15},{8,0},{9,1},... | collective-permute-start | bytes 294920 | tf_op jit(solution)/shard_map/ppermute | solution.py:20
  22.4 8.3 %collective-permute-start.7 = (bf16[128,384]{1,0:T(8,128)(2,1)S(1)}, bf16[128,384]{1,0:T(8,128)(2,1)S(1)}, u32[]{:S(2)}, u32[]{:S(2)}) collective-permute-start(bf16[128,384]{1,0:T(8,128)(2,1)S(1)} %twin_step.1.after.refs_0_), channel_id=1, source_target_pairs={{0,4},{1,5},{2,6},{3,7},{4,0},{5,1},{6,2},{7,3},{8,12},{9,13},{10,... | collective-permute-start | bytes 294920 | tf_op jit(solution)/shard_map/ppermute | solution.py:20
  23.3 7.3 %collective-permute-start.8 = (bf16[128,384]{1,0:T(8,128)(2,1)S(1)}, bf16[128,384]{1,0:T(8,128)(2,1)S(1)}, u32[]{:S(2)}, u32[]{:S(2)}) collective-permute-start(bf16[128,384]{1,0:T(8,128)(2,1)S(1)} %twin_step.1.after.refs_0_), channel_id=1, source_target_pairs={{0,12},{1,13},{2,14},{3,15},{4,8},{5,9},{6,10},{7,11},{8,4},{9,5},... | collective-permute-start | bytes 294920 | tf_op jit(solution)/shard_map/ppermute | solution.py:20
  23.9 8.5 %copy-start = (bf16[2,4096,64]{1,2,0:T(8,128)(2,1)S(1)}, bf16[2,4096,64]{1,2,0:T(8,128)(2,1)}, u32[]{:S(2)}) copy-start(bf16[2,4096,64]{1,2,0:T(8,128)(2,1)} %param.10) | copy-start | bytes 3145732
  31.1 1.4 %collective-permute-start.10 = (f32[64,384]{1,0:T(8,128)S(1)}, f32[64,384]{1,0:T(8,128)S(1)}, u32[]{:S(2)}, u32[]{:S(2)}) collective-permute-start(f32[64,384]{1,0:T(8,128)S(1)} %get-tuple-element.27), channel_id=1, source_target_pairs={{0,1},{1,0},{2,3},{3,2},{4,5},{5,4},{6,7},{7,6},{8,9},{9,8},{10,11... | collective-permute-start | bytes 294920 | tf_op jit(solution)/shard_map/ppermute | solution.py:20
